TPU v7x, 256 devices: a whole 4x4x8 slice. The times are simulated.
256 devices in a mesh: row: 16 (over z, y_lo), col: 16 (over y_hi, x, core).
Axes of the slice: x: 4, y: 4 (y_hi: 2, y_lo: 2; y = y_hi * 2 + y_lo), z: 8, core: 2. Of those that a mesh axis runs over, the one named last changes fastest.
Arguments:
- pair: bfloat16 [1536, 1536, 128], P('row', 'col'), may hold values from -6 to 6
- residue_mask: int32 [1536], replicated, may hold values 0 or 1
- norm_gain: float32 [128], replicated, may hold values from 0.1 to 1.9
- w_in: bfloat16 [128, 512], replicated, may hold values from -0.5 to 0.5
- b_in: float32 [512], replicated, may hold values from -3 to 3
- w_gate: bfloat16 [128, 128], replicated, may hold values from -0.5 to 0.5
- b_gate: float32 [128], replicated, may hold values from -3 to 3
- out_gain: float32 [128], replicated, may hold values from 0.1 to 1.9
- w_out: bfloat16 [128, 128], replicated, may hold values from -0.5 to 0.5
- b_out: float32 [128], replicated, may hold values from -3 to 3
Outputs:
- update: bfloat16 [1536, 1536, 128], P('row', 'col')
All inputs are finite; a program needn't handle non-finite values.
Results may differ from a plain program's by a relative error of at most 0.015.
Values may be sent and summed in bfloat16 or wider, within the bound.
A program may use at most 64 MiB of HBM per device.

v0:
```python
import jax
import jax.numpy as jnp
from jax import lax
from jax.sharding import PartitionSpec as P


def local(pair, residue_mask, norm_gain, w_in, b_in, w_gate, b_gate, out_gain, w_out, b_out):
    row_count, col_count, width = pair.shape
    channels = w_in.shape[1] // 4
    rows_total = lax.axis_size("row")
    cols_total = lax.axis_size("col")
    total = row_count * rows_total
    group = channels // cols_total
    repeat = max(1, rows_total // group)
    part = total // repeat
    row_index = lax.axis_index("row")
    col_index = lax.axis_index("col")
    valid = residue_mask.astype(jnp.float32)
    row_mask = lax.dynamic_slice_in_dim(valid, row_index * row_count, row_count)
    col_mask = lax.dynamic_slice_in_dim(valid, col_index * col_count, col_count)
    source = pair.astype(jnp.float32)
    mean = jnp.mean(source, axis=-1, keepdims=True)
    centred = source - mean
    var = jnp.mean(centred * centred, axis=-1, keepdims=True)
    normed = (centred * lax.rsqrt(var + 1e-05) * norm_gain).astype(jnp.bfloat16)
    proj = (
        jnp.einsum("ijd,de->eij", normed, w_in, preferred_element_type=jnp.float32)
        + b_in[:, None, None]
    )
    masked = row_mask[:, None] * col_mask[None, :]
    a_tile = (masked * jax.nn.sigmoid(proj[channels : 2 * channels]) * proj[:channels]).astype(
        jnp.bfloat16
    )
    b_tile = (
        masked * jax.nn.sigmoid(proj[3 * channels :]) * proj[2 * channels : 3 * channels]
    ).astype(jnp.bfloat16)
    a_group, b_group = (
        lax.all_to_all(a_tile, "col", split_axis=0, concat_axis=2, tiled=True),
        lax.all_to_all(b_tile, "col", split_axis=0, concat_axis=2, tiled=True),
    )
    a_rep = jnp.repeat(a_group, repeat, axis=0)
    b_rep = jnp.repeat(b_group, repeat, axis=0)
    a_full, b_full = (
        lax.all_to_all(a_rep, "row", split_axis=0, concat_axis=1, tiled=True),
        lax.all_to_all(b_rep, "row", split_axis=0, concat_axis=1, tiled=True),
    )
    start = row_index % repeat * part
    b_part = lax.dynamic_slice_in_dim(b_full, start, part, 1)
    partial_value = jnp.einsum("cik,cjk->cij", a_full, b_part, preferred_element_type=jnp.float32)
    returned = lax.all_to_all(
        partial_value.astype(jnp.bfloat16), "row", split_axis=1, concat_axis=0, tiled=True
    ).astype(partial_value.dtype)
    grouped = (
        returned.reshape(group, repeat, row_count, part)
        .transpose(0, 2, 1, 3)
        .reshape(group, row_count, total)
    )
    prod = lax.all_to_all(
        grouped.astype(jnp.bfloat16), "col", split_axis=2, concat_axis=0, tiled=True
    ).astype(grouped.dtype)
    prod_mean = jnp.mean(prod, axis=0, keepdims=True)
    prod_centred = prod - prod_mean
    prod_var = jnp.mean(prod_centred * prod_centred, axis=0, keepdims=True)
    prod_norm = (prod_centred * lax.rsqrt(prod_var + 1e-05) * out_gain[:, None, None]).astype(
        jnp.bfloat16
    )
    linear = jnp.einsum("cij,ce->ije", prod_norm, w_out, preferred_element_type=jnp.float32) + b_out
    gating = jax.nn.sigmoid(
        jnp.einsum("ijd,de->ije", normed, w_gate, preferred_element_type=jnp.float32) + b_gate
    )
    return (gating * linear).astype(jnp.bfloat16)


def solution(mesh):
    in_specs = (P("row", "col", None), P(), P(), P(), P(), P(), P(), P(), P(), P())
    out_specs = P("row", "col", None)
    return jax.shard_map(local, mesh=mesh, in_specs=in_specs, out_specs=out_specs, check_vma=False)
```

profile of v0, /device:TPU:1, one launch (start us, length us, event | category | flops | bytes accessed | tf_op | source)
XLA Modules:
  0.0 584.9 jit_solution(1296190321457291279)
XLA Ops:
  14.9 4.8 copy.40
  19.7 8.4 %all-to-all-start.2 = ((bf16[128,96,96]{2,1,0:T(8,128)(2,1)}), bf16[128,96,96]{2,1,0:T(8,128)(2,1)}, u32[]{:S(2)}, u32[]{:S(2)}) async-start(bf16[128,96,96]{2,1,0:T(8,128)(2,1)} %copy.40), calls=%async_computation.2 | async-start | bytes 6291456 | tf_op jit(solution)/shard_map/all_to_all | solution.py:39
  28.1 4.8 copy.38
  32.9 37.1 %all-to-all-done.2 = bf16[128,96,96]{2,1,0:T(8,128)(2,1)} async-done(((bf16[128,96,96]{2,1,0:T(8,128)(2,1)}), bf16[128,96,96]{2,1,0:T(8,128)(2,1)}, u32[]{:S(2)}, u32[]{:S(2)}) %all-to-all-start.2) | async-done | bytes 2359328 | tf_op jit(solution)/shard_map/all_to_all | solution.py:39
  70.0 6.4 %all-to-all-start = ((bf16[128,96,96]{2,1,0:T(8,128)(2,1)}), bf16[128,96,96]{2,1,0:T(8,128)(2,1)}, u32[]{:S(2)}, u32[]{:S(2)}) async-start(bf16[128,96,96]{2,1,0:T(8,128)(2,1)} %copy.38), calls=%async_computation | async-start | bytes 6291456 | tf_op jit(solution)/shard_map/all_to_all | solution.py:38
  76.4 5.6 copy.41
  82.0 6.4 %all_to_all.64 = bf16[8,96,1536]{2,1,0:T(8,128)(2,1)} reshape(bf16[8,96,16,96]{3,2,1,0:T(8,128)(2,1)} %copy.41) | data formatting | bytes 4718592 | tf_op jit(solution)/shard_map/all_to_all | solution.py:39
  88.4 29.9 %all-to-all-done = bf16[128,96,96]{2,1,0:T(8,128)(2,1)} async-done(((bf16[128,96,96]{2,1,0:T(8,128)(2,1)}), bf16[128,96,96]{2,1,0:T(8,128)(2,1)}, u32[]{:S(2)}, u32[]{:S(2)}) %all-to-all-start) | async-done | bytes 2359328 | tf_op jit(solution)/shard_map/all_to_all | solution.py:38
  122.7 8.5 %all-to-all-start.3 = ((bf16[16,96,1536]{2,1,0:T(8,128)(2,1)}), bf16[16,96,1536]{2,1,0:T(8,128)(2,1)}, u32[]{:S(2)}, u32[]{:S(2)}) async-start(bf16[16,96,1536]{2,1,0:T(8,128)(2,1)} %bitcast.52), calls=%async_computation.3 | async-start | bytes 9437184 | tf_op jit(solution)/shard_map/all_to_all | solution.py:45
  131.2 5.6 copy.39
  136.7 6.4 %all_to_all.29 = bf16[8,96,1536]{2,1,0:T(8,128)(2,1)} reshape(bf16[8,96,16,96]{3,2,1,0:T(8,128)(2,1)} %copy.39) | data formatting | bytes 4718592 | tf_op jit(solution)/shard_map/all_to_all | solution.py:38
  143.1 96.7 %all-to-all-done.3 = bf16[16,96,1536]{2,1,0:T(8,128)(2,1)} async-done(((bf16[16,96,1536]{2,1,0:T(8,128)(2,1)}), bf16[16,96,1536]{2,1,0:T(8,128)(2,1)}, u32[]{:S(2)}, u32[]{:S(2)}) %all-to-all-start.3) | async-done | bytes 4718624 | tf_op jit(solution)/shard_map/all_to_all | solution.py:45
  244.2 5.2 all-to-all-start.1
  249.4 107.8 %all-to-all-done.1 = bf16[16,96,1536]{2,1,0:T(8,128)(2,1)} async-done(((bf16[16,96,1536]{2,1,0:T(8,128)(2,1)}), bf16[16,96,1536]{2,1,0:T(8,128)(2,1)}, u32[]{:S(2)}, u32[]{:S(2)}) %all-to-all-start.1) | async-done | bytes 4718624 | tf_op jit(solution)/shard_map/all_to_all | solution.py:44
  357.2 7.0 %fusion.20 = bf16[1,1536,768]{2,1,0:T(8,128)(2,1)S(1)} fusion(bf16[1536,1536]{1,0:T(8,128)(2,1)} %bitcast.6, bf16[1,1536,1536]{2,1,0:T(8,128)(2,1)} %bitcast.10, s32[]{:T(128)S(6)} %select_n.19), kind=kOutput, calls=%fused_computation.31 | convolution fusion | flops 3625058304 | bytes 9437188 | tf_op jit(solution)/shard_map/cik,cjk->cij/dot_general | solution.py:49
  364.1 33.8 %copy.54 = bf16[1,1536,768]{2,0,1:T(2,128)(2,1)} copy(bf16[1,1536,768]{2,1,0:T(8,128)(2,1)S(1)} %fusion.20) | data formatting | bytes 4718592 | tf_op jit(solution)/shard_map/convert_element_type | solution.py:51
  398.5 25.5 %reduce.2 = bf16[1536,768]{1,0:T(8,128)(2,1)} reduce(bf16[1536,1,768]{2,1,0:T(2,128)(2,1)} %bitcast.53, bf16[]{:T(256)} %broadcast.81), dimensions={1}, to_apply=%bitcast.49.reduce_sub_computation | reduce | bytes 4718594
  428.1 59.3 %all_to_all.75 = bf16[16,2,36864]{2,1,0:T(2,128)(2,1)} all-to-all(bf16[16,2,36864]{2,1,0:T(2,128)(2,1)} %reshape.102), channel_id=1, replica_groups=mesh['row'=16,'col'=16] {'row'}, dimensions={0} | all-to-all | bytes 4718592 | tf_op jit(solution)/shard_map/all_to_all | solution.py:50
  487.4 10.7 %reshape.103 = bf16[1536,1,768]{2,1,0:T(2,128)(2,1)} reshape(bf16[16,2,36864]{2,1,0:T(2,128)(2,1)} %all_to_all.75) | data formatting | bytes 4718592
  502.2 4.9 copy.48
  507.1 51.1 %all_to_all.76 = bf16[8,96,1536]{1,0,2:T(8,128)(2,1)} all-to-all(bf16[8,96,1536]{1,0,2:T(8,128)(2,1)} %bitcast.55), channel_id=1, replica_groups=mesh['row'=16,'col'=16] {'col'}, dimensions={2} | all-to-all | bytes 4718592 | tf_op jit(solution)/shard_map/all_to_all | solution.py:58
  558.2 4.8 copy.45
  563.0 6.3 %reshape.98 = f32[8,96,16,96]{3,2,1,0:T(8,128)} reshape(bf16[8,96,1536]{2,1,0:T(8,128)(2,1)} %copy.45) | data formatting | bytes 7077888 | tf_op jit(solution)/shard_map/convert_element_type | solution.py:60
  579.4 5.5 multiply_convert_fusion
  (43 shorter events, 42.3 us)
Async XLA Ops:
  0.0 8.0 %copy-start = (bf16[128,512]{1,0:T(8,128)(2,1)S(1)}, bf16[128,512]{1,0:T(8,128)(2,1)}, u32[]{:S(2)}) copy-start(bf16[128,512]{1,0:T(8,128)(2,1)} %param.13) | copy-start | bytes 393220
  0.0 8.0 %copy-start.3 = (bf16[96,96,128]{2,1,0:T(8,128)(2,1)S(1)}, bf16[96,96,128]{2,1,0:T(8,128)(2,1)}, u32[]{:S(2)}) copy-start(bf16[96,96,128]{2,1,0:T(8,128)(2,1)} %param.10) | copy-start | bytes 7077892
  0.0 8.0 %copy-start.6 = (f32[128]{0:T(128)S(1)}, f32[128]{0:T(128)}, u32[]{:S(2)}) copy-start(f32[128]{0:T(128)} %param.12) | copy-start | bytes 1540
  0.0 8.1 %copy-start.5 = (f32[512]{0:T(512)S(1)}, f32[512]{0:T(512)}, u32[]{:S(2)}) copy-start(f32[512]{0:T(512)} %param.14) | copy-start | bytes 6148
  19.7 50.4 %all-to-all-start.2 = ((bf16[128,96,96]{2,1,0:T(8,128)(2,1)}), bf16[128,96,96]{2,1,0:T(8,128)(2,1)}, u32[]{:S(2)}, u32[]{:S(2)}) async-start(bf16[128,96,96]{2,1,0:T(8,128)(2,1)} %copy.40), calls=%async_computation.2 | async-start | bytes 6291456 | tf_op jit(solution)/shard_map/all_to_all | solution.py:39
  70.0 48.3 %all-to-all-start = ((bf16[128,96,96]{2,1,0:T(8,128)(2,1)}), bf16[128,96,96]{2,1,0:T(8,128)(2,1)}, u32[]{:S(2)}, u32[]{:S(2)}) async-start(bf16[128,96,96]{2,1,0:T(8,128)(2,1)} %copy.38), calls=%async_computation | async-start | bytes 6291456 | tf_op jit(solution)/shard_map/all_to_all | solution.py:38
  122.7 117.1 %all-to-all-start.3 = ((bf16[16,96,1536]{2,1,0:T(8,128)(2,1)}), bf16[16,96,1536]{2,1,0:T(8,128)(2,1)}, u32[]{:S(2)}, u32[]{:S(2)}) async-start(bf16[16,96,1536]{2,1,0:T(8,128)(2,1)} %bitcast.52), calls=%async_computation.3 | async-start | bytes 9437184 | tf_op jit(solution)/shard_map/all_to_all | solution.py:45
  244.2 113.0 %all-to-all-start.1 = ((bf16[16,96,1536]{2,1,0:T(8,128)(2,1)}), bf16[16,96,1536]{2,1,0:T(8,128)(2,1)}, u32[]{:S(2)}, u32[]{:S(2)}) async-start(bf16[16,96,1536]{2,1,0:T(8,128)(2,1)} %bitcast.51), calls=%async_computation.1 | async-start | bytes 9437184 | tf_op jit(solution)/shard_map/all_to_all | solution.py:44
  569.3 4.6 copy-start.2
  574.9 2.0 copy-start.7
  577.0 0.9 copy-start.4
  577.9 1.5 copy-start.8
  577.9 1.5 copy-start.9
  577.9 1.5 copy-start.10
  579.4 5.5 copy-start.1
where the time goes:
time: 587 us; the launch traced here: 585 us
  waiting for transfers between devices  271 us (46%)
  local copies, waits for them, and re-layouts  115 us (20%)
  blocking collectives  110 us (19%)
  other arithmetic  42.9 us (7%)
  starting transfers between devices  28.5 us (5%)
  matrix products  16.6 us (3%)
    all_to_all x1, waiting for transfers between devices, local(): lax.all_to_all(a_rep, 'row', split_axis=0, concat_axis=1, tiled=True)  108 us
    all_to_all x1, waiting for transfers between devices, local(): lax.all_to_all(b_rep, 'row', split_axis=0, concat_axis=1, tiled=True)  96.7 us
    all_to_all x1, blocking collectives, local(): lax.all_to_all(partial_value.astype(jnp.bfloat16), 'row', split_axis=1, c...  59.3 us
    all_to_all x1, blocking collectives, local(): lax.all_to_all(grouped.astype(jnp.bfloat16), 'col', split_axis=2, concat_...  51.1 us
    all_to_all x1, waiting for transfers between devices, local(): lax.all_to_all(b_tile, 'col', split_axis=0, concat_axis=2, tiled=True)  37.1 us
    convert_element_type x1, local copies, waits for them, and re-layouts, local(): partial_value.astype(jnp.bfloat16)  33.8 us
    all_to_all x1, waiting for transfers between devices, local(): lax.all_to_all(a_tile, 'col', split_axis=0, concat_axis=2, tiled=True)  29.9 us
    unnamed x1, other arithmetic  25.5 us
  transfers between devices with their start and end apart: 4, of which 4 were waited for; matrix products, arithmetic and copies ran while one was open for 3% of the time, Pallas kernels for 0%

commit v1 on v0

v1 whole, which is shorter than its diff:
```python
import functools

import jax
import jax.numpy as jnp
from jax import lax
from jax.experimental import pallas as pl
from jax.experimental.pallas import tpu as pltpu
from jax.sharding import PartitionSpec as P

MESH = pl.DeviceIdType.MESH
BF16 = jnp.bfloat16
F32 = jnp.float32
LANES = 128


def join4(parts):
    lane = lax.broadcasted_iota(jnp.int32, parts[0].shape, 1)
    one, two, three = (pltpu.roll(parts[n], 128 - 32 * n, 1) for n in (1, 2, 3))
    return (
        jnp.where(lane < 96, parts[0], one),
        jnp.where(lane < 64, one, two),
        jnp.where(lane < 32, two, three),
    )


def split4(parts):
    lane = lax.broadcasted_iota(jnp.int32, parts[0].shape, 1)
    first, second, third = parts
    return (
        first,
        jnp.where(lane < 32, pltpu.roll(first, 32, 1), pltpu.roll(second, 32, 1)),
        jnp.where(lane < 64, pltpu.roll(second, 64, 1), pltpu.roll(third, 64, 1)),
        pltpu.roll(third, 96, 1),
    )


def triangle_kernel(
    nz, nch, ci, ab, out, recv1, zs, za, zb, other, prods, back, un, s1, r1, s2, r2a, r2b, so, ro, s3, r3, s4, r4
):
    nq = 2 * nz
    row, col = lax.axis_index("row"), lax.axis_index("col")
    z, yl = row // 2, row % 2
    w, core = col // 2, col % 2
    mine = yl * nz + w

    barrier = pltpu.get_barrier_semaphore()

    def greet_plane(t, _):
        dev = lax.rem(yl * nq + col + t, 2 * nq)
        pl.semaphore_signal(
            barrier, inc=1, device_id=(2 * z + dev // nq, dev % nq), device_id_type=MESH
        )
        return 0

    lax.fori_loop(1, 2 * nq, greet_plane, 0)

    def greet_line(t, _):
        pl.semaphore_signal(
            barrier, inc=1, device_id=(2 * lax.rem(z + t, nz) + yl, col), device_id_type=MESH
        )
        return 0

    lax.fori_loop(1, nz, greet_line, 0)
    pl.semaphore_wait(barrier, 2 * nq - 1 + nz - 1)

    def send1(arr, m):
        def step(t, _):
            p = lax.rem(mine + t, nq)
            here = jnp.logical_and(p == mine, core == yl)

            @pl.when(here)
            def _():
                pltpu.make_async_copy(ab.at[arr, m, p], recv1.at[arr, m, col], r1.at[arr, m]).start()

            @pl.when(jnp.logical_not(here))
            def _():
                pltpu.make_async_remote_copy(
                    src_ref=ab.at[arr, m, p],
                    dst_ref=recv1.at[arr, m, col],
                    send_sem=s1,
                    recv_sem=r1.at[arr, m],
                    device_id=(2 * z + p // nz, 2 * (p % nz) + yl),
                    device_id_type=MESH,
                ).start()

            return 0

        lax.fori_loop(0, nq, step, 0)

    def wait_all(ref, sem):
        pltpu.make_async_copy(ref, ref, sem).wait()

    def send_line(src, dst, target, send_sem, recv_sem):
        @pl.when(target == z)
        def _():
            pltpu.make_async_copy(src, dst, recv_sem).start()

        @pl.when(target != z)
        def _():
            pltpu.make_async_remote_copy(
                src_ref=src,
                dst_ref=dst,
                send_sem=send_sem,
                recv_sem=recv_sem,
                device_id=(2 * target + yl, col),
                device_id_type=MESH,
            ).start()

    def join_and_send(arr, m):
        def step(t, _):
            ch = lax.rem(z + 1 + t, nz)
            for g in range(nq // 4):
                blocks = join4([recv1[arr, m, 4 * g + n, ch].astype(F32) for n in range(4)])
                for n in range(3):
                    zs[arr, m, ch, :, (3 * g + n) * LANES : (3 * g + n + 1) * LANES] = blocks[
                        n
                    ].astype(BF16)
            if arr == 0:
                send_line(zs.at[0, m, ch], za.at[m, z], ch, s2, r2a.at[m])
            else:
                send_line(zs.at[1, m, ch], zb.at[z, m * ci : (m + 1) * ci], ch, s2, r2b)
            return 0

        lax.fori_loop(0, nz, step, 0)

    order = [(1, m) for m in range(nch)] + [(0, m) for m in range(nch)]
    send1(*order[0])
    send1(*order[1])
    for n, (arr, m) in enumerate(order):
        wait_all(recv1.at[arr, m], r1.at[arr, m])
        if n + 2 < len(order):
            send1(*order[n + 2])
        join_and_send(arr, m)

    ti = nch * ci
    wait_all(zb, r2b)

    def multiply(lhs_ref, m, h):
        lhs = lhs_ref[...].reshape(nz * ci, lhs_ref.shape[-1])

        def step(g, _):
            rhs = zb[pl.ds(4 * g, 4)].reshape(4 * ti, zb.shape[-1])
            res = lax.dot_general(lhs, rhs, (((1,), (1,)), ((), ())), preferred_element_type=F32)
            prods[m, :, h, g] = res.reshape(nz, ci, 4 * ti).astype(BF16)
            return 0

        lax.fori_loop(0, nz // 4, step, 0)

    def swap(m):
        return pltpu.make_async_remote_copy(
            src_ref=za.at[m],
            dst_ref=other.at[m],
            send_sem=so.at[m],
            recv_sem=ro.at[m],
            device_id=(row, 2 * w + 1 - core),
            device_id_type=MESH,
        )

    def send_products(m):
        def step(t, _):
            target = lax.rem(z + 1 + t, nz)
            send_line(prods.at[m, target], back.at[m, z], target, s3, r3.at[m])
            return 0

        lax.fori_loop(0, nz, step, 0)

    def split_and_send(m):
        wait_all(back.at[m], r3.at[m])

        def step(ch, _):
            for h in range(2):
                for g in range(nz // 4):
                    blocks = split4(
                        [
                            back[m, ch, h, g, :, n * LANES : (n + 1) * LANES].astype(F32)
                            for n in range(3)
                        ]
                    )
                    for n in range(4):
                        un[m, h * nz + 4 * g + n, ch] = blocks[n].astype(BF16)
            return 0

        lax.fori_loop(0, nz, step, 0)

        def send(t, _):
            p = lax.rem(mine + 1 + t, nq)

            @pl.when(p == mine)
            def _():
                pltpu.make_async_copy(un.at[m, p], out.at[m, mine], r4.at[m]).start()

            @pl.when(p != mine)
            def _():
                pltpu.make_async_remote_copy(
                    src_ref=un.at[m, p],
                    dst_ref=out.at[m, mine],
                    send_sem=s4,
                    recv_sem=r4.at[m],
                    device_id=(2 * z + p // nz, 2 * (p % nz) + core),
                    device_id_type=MESH,
                ).start()

            return 0

        lax.fori_loop(0, nq, send, 0)

    for m in range(nch):
        wait_all(za.at[m], r2a.at[m])
        swap(m).start()
        multiply(za.at[m], m, core)
        swap(m).wait_recv()
        multiply(other.at[m], m, 1 - core)
        send_products(m)
        if m:
            split_and_send(m - 1)
    split_and_send(nch - 1)
    for m in range(nch):
        wait_all(out.at[m], r4.at[m])

    for arr in range(2):
        for m in range(nch):

            @pl.when(core == yl)
            def _():
                wait_all(ab.at[arr, m, 0 : nq - 1], s1)

            @pl.when(core != yl)
            def _():
                wait_all(ab.at[arr, m], s1)

            wait_all(zs.at[arr, m, 0 : nz - 1], s2)
    for m in range(nch):
        swap(m).wait_send()
        wait_all(prods.at[m, 0 : nz - 1], s3)
        wait_all(un.at[m, 0 : nq - 1], s4)


def exchange(ab, nz):
    _, nch, nq, _, ci, _ = ab.shape
    ti = nch * ci
    depth = nq * ti
    sem = pltpu.SemaphoreType.DMA
    vmem = pl.BlockSpec(memory_space=pltpu.VMEM)
    return pl.pallas_call(
        functools.partial(triangle_kernel, nz, nch, ci),
        out_shape=jax.ShapeDtypeStruct((nch, nq, nz, ci, LANES), BF16),
        in_specs=[vmem],
        out_specs=vmem,
        scratch_shapes=[
            pltpu.VMEM((2, nch, nq, nz, ci, LANES), BF16),
            pltpu.VMEM((2, nch, nz, ci, depth), BF16),
            pltpu.VMEM((nch, nz, ci, depth), BF16),
            pltpu.VMEM((nz, ti, depth), BF16),
            pltpu.VMEM((nch, nz, ci, depth), BF16),
            pltpu.VMEM((nch, nz, 2, nz // 4, ci, 4 * ti), BF16),
            pltpu.VMEM((nch, nz, 2, nz // 4, ci, 4 * ti), BF16),
            pltpu.VMEM((nch, nq, nz, ci, LANES), BF16),
            sem,
            sem((2, nch)),
            sem,
            sem((nch,)),
            sem,
            sem((nch,)),
            sem((nch,)),
            sem,
            sem((nch,)),
            sem,
            sem((nch,)),
        ],
        compiler_params=pltpu.CompilerParams(
            collective_id=0, has_side_effects=True, vmem_limit_bytes=56 * 2**20
        ),
    )(ab)


def local(pair, residue_mask, norm_gain, w_in, b_in, w_gate, b_gate, out_gain, w_out, b_out):
    ti, tj, _ = pair.shape
    channels = w_in.shape[1] // 4
    nz = lax.axis_size("row") // 2
    nq = 2 * nz
    ci = 32
    nch = ti // ci
    row_index = lax.axis_index("row")
    col_index = lax.axis_index("col")
    valid = residue_mask.astype(F32)
    row_mask = lax.dynamic_slice_in_dim(valid, row_index * ti, ti)
    col_mask = lax.dynamic_slice_in_dim(valid, col_index * tj, tj)
    source = pair.astype(F32)
    mean = jnp.mean(source, axis=-1, keepdims=True)
    centred = source - mean
    var = jnp.mean(centred * centred, axis=-1, keepdims=True)
    normed = (centred * lax.rsqrt(var + 1e-05) * norm_gain).astype(BF16)
    proj = (
        jnp.einsum("ijd,de->eij", normed, w_in, preferred_element_type=F32) + b_in[:, None, None]
    )
    masked = row_mask[:, None] * col_mask[None, :]
    a_tile = masked * jax.nn.sigmoid(proj[channels : 2 * channels]) * proj[:channels]
    b_tile = masked * jax.nn.sigmoid(proj[3 * channels :]) * proj[2 * channels : 3 * channels]
    ab = jnp.stack([a_tile, b_tile]).astype(BF16)
    ab = jnp.pad(ab, ((0, 0), (0, 0), (0, 0), (0, LANES - tj)))
    ab = ab.reshape(2, nq, nz, nch, ci, LANES).transpose(0, 3, 1, 2, 4, 5)
    moved = exchange(ab, nz)
    prod = moved.transpose(1, 2, 0, 3, 4).reshape(channels, ti, LANES)[:, :, :tj].astype(F32)
    prod_mean = jnp.mean(prod, axis=0, keepdims=True)
    prod_centred = prod - prod_mean
    prod_var = jnp.mean(prod_centred * prod_centred, axis=0, keepdims=True)
    prod_norm = (prod_centred * lax.rsqrt(prod_var + 1e-05) * out_gain[:, None, None]).astype(BF16)
    linear = jnp.einsum("cij,ce->ije", prod_norm, w_out, preferred_element_type=F32) + b_out
    gating = jax.nn.sigmoid(
        jnp.einsum("ijd,de->ije", normed, w_gate, preferred_element_type=F32) + b_gate
    )
    return (gating * linear).astype(BF16)


def solution(mesh):
    in_specs = (P("row", "col", None), P(), P(), P(), P(), P(), P(), P(), P(), P())
    out_specs = P("row", "col", None)
    return jax.shard_map(local, mesh=mesh, in_specs=in_specs, out_specs=out_specs, check_vma=False)
```

time: 587 us -> 246 us (0.42)
  waiting for transfers between devices: 271 us -> 0 us
  Pallas kernels: 0 us -> 200 us
  blocking collectives: 110 us -> 0 us
  local copies, waits for them, and re-layouts: 115 us -> 19.5 us
  starting transfers between devices: 28.5 us -> 0 us
  other arithmetic: 42.9 us -> 16.1 us
  matrix products: 16.6 us -> 9.61 us
    all_to_all x4 -> x0, waiting for transfers between devices: 271 us -> none  [the longest x1 108 us: local(): lax.all_to_all(a_rep, 'row', split_axis=0, concat_axis=1, tiled=True)]
    pallas_call x0 -> x1, Pallas kernels: none -> 200 us  [exchange(): pl.pallas_call(functools.partial(triangle_kernel, nz, nch, ci), out_shape...]
    all_to_all x2 -> x0, blocking collectives: 110 us -> none  [the longest x1 59.3 us: local(): lax.all_to_all(partial_value.astype(jnp.bfloat16), 'row', split_axis=1, c...]
    convert_element_type x6 -> x0, local copies, waits for them, and re-layouts: 56.6 us -> none  [the longest x1 33.8 us: local(): partial_value.astype(jnp.bfloat16)]
    all_to_all x5 -> x0, local copies, waits for them, and re-layouts: 28.7 us -> none  [the longest x2 12 us: local(): lax.all_to_all(b_tile, 'col', split_axis=0, concat_axis=2, tiled=True)]
    all_to_all x4 -> x0, starting transfers between devices: 28.5 us -> none  [the longest x1 8.46 us: local(): lax.all_to_all(b_rep, 'row', split_axis=0, concat_axis=1, tiled=True)]
    unnamed x1 -> x0, other arithmetic: 25.5 us -> none
    unnamed x26 -> x19, local copies, waits for them, and re-layouts: 20.6 us -> 8.45 us
  transfers between devices with their start and end apart: 4 -> 0, of which waited for: 4 -> 0; matrix products, arithmetic and copies ran while one was open for 3% -> 0% of each run, Pallas kernels for 0% -> 0%
where the time goes in v1:
time: 246 us; the launch traced here: 245 us
  Pallas kernels  200 us (81%)
  local copies, waits for them, and re-layouts  19.5 us (8%)
  other arithmetic  16.1 us (7%)
  matrix products  9.61 us (4%)
    pallas_call x1, Pallas kernels, exchange(): pl.pallas_call(functools.partial(triangle_kernel, nz, nch, ci), out_shape...  200 us
    unnamed x19, local copies, waits for them, and re-layouts  8.45 us
    dot_general x1, matrix products, local(): jnp.einsum('ijd,de->ije', normed, w_gate, preferred_element_type=F32)  5.52 us
    another operation x2, other arithmetic, local(): ab = jnp.stack([a_tile, b_tile]).astype(BF16)  5.46 us

profile of v1, /device:TPU:1, one launch (start us, length us, event | category | flops | bytes accessed | tf_op | source)
XLA Modules:
  0.0 245.2 jit_solution(9259344528933600485)
XLA Ops:
  0.0 0.8 convert_element_type.23
  0.9 0.1 fusion.29
  1.0 0.1 broadcast_multiply_fusion
  1.0 2.6 %convert_reduce_fusion.1 = f32[96,96]{1,0:T(8,128)S(1)} fusion(bf16[96,96,128]{2,1,0:T(8,128)(2,1)} %param.10), kind=kLoop, calls=%fused_computation.10 | loop fusion | flops 2350080 | bytes 2396160 | tf_op jit(solution)/shard_map/reduce_sum | solution.py:289
  3.6 4.4 %fusion.7 = f32[96,96]{1,0:T(8,128)S(1)} fusion(bf16[96,96,128]{2,1,0:T(8,128)(2,1)} %param.10, f32[96,96]{1,0:T(8,128)S(1)} %broadcast_multiply_fusion.2), kind=kLoop, calls=%fused_computation.13 | loop fusion | flops 4709376 | bytes 2433024 | tf_op jit(solution)/shard_map/reduce_sum | solution.py:291
  8.1 2.7 %add_bitcast_fusion = f32[512,96,96]{0,2,1:T(8,128)S(1)} fusion(f32[512]{0:T(512)S(1)} %copy-done.3, bf16[96,96,128]{2,1,0:T(8,128)(2,1)S(1)} %copy-done.1, f32[128]{0:T(128)S(1)} %copy-done.4, f32[96,96]{1,0:T(8,128)S(1)} %add_rsqrt_fusion.1, f32[96,96]{1,0:T(8,128)S(1)} %broadcast_multiply_fusion.2, bf16[128,512]{1,0:T(8,128)(2,1)S(1)} %copy-done), kind=kOutput, calls=%fused_computation | convolution fusion | flops 1218576384 | bytes 21441024 | tf_op jit(solution)/shard_map/ijd,de->eij/dot_general | solution.py:294
  10.7 2.8 %fusion.22 = (bf16[1,128,96,96]{1,3,2,0:T(8,128)(2,1)S(1)}, bf16[1,128,96,96]{1,3,2,0:T(8,128)(2,1)S(1)}) fusion(f32[512,96,96]{0,2,1:T(8,128)S(1)} %add_bitcast_fusion, f32[96,96]{1,0:T(8,128)S(1)} %broadcast_multiply_fusion), kind=kLoop, calls=%fused_computation.34 | loop fusion | flops 14155776 | bytes 23629824 | tf_op jit(solution)/shard_map/stack | solution.py:299
  13.6 2.6 %pad_maximum_fusion = bf16[2,128,96,96]{1,3,2,0:T(8,128)(2,1)} fusion(bf16[1,128,96,96]{1,3,2,0:T(8,128)(2,1)S(1)} %get-tuple-element.6, bf16[1,128,96,96]{1,3,2,0:T(8,128)(2,1)S(1)} %get-tuple-element.5), kind=kLoop, calls=%fused_computation.30 | loop fusion | flops 2359296 | bytes 9437184 | tf_op jit(solution)/shard_map/stack | solution.py:299
  16.2 8.4 %copy.15 = bf16[2,128,96,96]{3,2,1,0:T(8,128)(2,1)} copy(bf16[2,128,96,96]{1,3,2,0:T(8,128)(2,1)} %pad_maximum_fusion) | data formatting | bytes 9437184
  24.6 4.0 %pad.4.clone = bf16[2,128,96,128]{3,2,1,0:T(8,128)(2,1)S(1)} pad(bf16[2,128,96,96]{3,2,1,0:T(8,128)(2,1)} %copy.15, bf16[]{:T(256)} %constant.29.clone.1), padding=0_0x0_0x0_0x0_32 | pad | bytes 11010050 | tf_op jit(solution)/shard_map/jit(_pad)/pad | solution.py:300
  28.6 4.5 %copy.19 = bf16[2,16,8,3,32,128]{5,4,2,1,3,0:T(8,128)(2,1)} copy(bf16[2,16,8,3,32,128]{5,4,3,2,1,0:T(8,128)(2,1)S(1)} %bitcast.24) | data formatting | bytes 12582912 | tf_op jit(solution)/shard_map/reshape | solution.py:301
  33.2 199.7 %shard_map.100 = bf16[3,16,8,32,128]{4,3,2,1,0:T(8,128)(2,1)} custom-call(bf16[2,3,16,8,32,128]{5,4,3,2,1,0:T(8,128)(2,1)} %bitcast.25), custom_call_target="tpu_custom_call" | custom-call | tf_op jit(solution)/shard_map/pallas_call | solution.py:244
  232.9 2.5 %copy.13 = bf16[16,8,3,32,128]{4,3,2,1,0:T(8,128)(2,1)S(1)} copy(bf16[16,8,3,32,128]{4,3,1,0,2:T(8,128)(2,1)} %bitcast.26) | data formatting | bytes 6291456 | tf_op jit(solution)/shard_map/transpose | solution.py:303
  235.3 0.0 copy-start.5
  235.3 0.7 convert_reduce_fusion
  236.0 0.0 copy-start.2
  236.0 1.1 fusion.2
  237.1 1.0 fusion.4
  238.2 0.0 copy-done.2
  238.2 0.0 copy-start.6
  238.2 0.0 copy-start.7
  238.2 0.0 copy-start.8
  238.2 1.4 fusion.20
  239.7 5.5 %multiply_convert_fusion = bf16[96,96,128]{2,1,0:T(8,128)(2,1)} fusion(f32[96,96,128]{2,1,0:T(8,128)S(1)} %fusion.20, f32[128]{0:T(128)S(1)} %copy-done.7, f32[128]{0:T(128)S(1)} %copy-done.8, bf16[96,96,128]{2,1,0:T(8,128)(2,1)S(1)} %copy-done.1, f32[128]{0:T(128)S(1)} %copy-done.4, f32[96,96]{1,0:T(8,128)S(1)} %add_rsqrt_fusion.1, ...), kind=kOutput, calls=%fused_computation.31 | convolution fusion | flops 316145664 | bytes 9545216 | tf_op jit(solution)/shard_map/ijd,de->ije/dot_general | solution.py:310
  (16 shorter events, 0.1 us)
Async XLA Ops:
  0.0 8.0 %copy-start = (bf16[128,512]{1,0:T(8,128)(2,1)S(1)}, bf16[128,512]{1,0:T(8,128)(2,1)}, u32[]{:S(2)}) copy-start(bf16[128,512]{1,0:T(8,128)(2,1)} %param.13) | copy-start | bytes 393220
  0.0 8.0 %copy-start.1 = (bf16[96,96,128]{2,1,0:T(8,128)(2,1)S(1)}, bf16[96,96,128]{2,1,0:T(8,128)(2,1)}, u32[]{:S(2)}) copy-start(bf16[96,96,128]{2,1,0:T(8,128)(2,1)} %param.10) | copy-start | bytes 7077892
  0.0 8.0 %copy-start.4 = (f32[128]{0:T(128)S(1)}, f32[128]{0:T(128)}, u32[]{:S(2)}) copy-start(f32[128]{0:T(128)} %param.12) | copy-start | bytes 1540
  0.0 8.0 %copy-start.3 = (f32[512]{0:T(512)S(1)}, f32[512]{0:T(512)}, u32[]{:S(2)}) copy-start(f32[512]{0:T(512)} %param.14) | copy-start | bytes 6148
  235.3 1.8 copy-start.5
  236.0 2.1 copy-start.2
  238.2 1.5 copy-start.6
  238.2 1.5 copy-start.7
  238.2 1.5 copy-start.8

commit v2 on v1

--- a/solution.py
+++ b/solution.py
@@ -11,6 +11,7 @@
 BF16 = jnp.bfloat16
 F32 = jnp.float32
 LANES = 128
+CHUNK = 32
 
 
 def join4(parts):
@@ -34,8 +35,51 @@
     )
 
 
+def sigmoid(x):
+    return 0.5 * jnp.tanh(0.5 * x) + 0.5
+
+
 def triangle_kernel(
-    nz, nch, ci, ab, out, recv1, zs, za, zb, other, prods, back, un, s1, r1, s2, r2a, r2b, so, ro, s3, r3, s4, r4
+    nz,
+    nch,
+    ci,
+    pair,
+    mask,
+    norm_gain,
+    w_in,
+    b_in,
+    w_gate,
+    b_gate,
+    out_gain,
+    w_out,
+    b_out,
+    update,
+    nrm,
+    wt,
+    bias,
+    gate,
+    flip,
+    ab,
+    recv1,
+    zs,
+    za,
+    zb,
+    other,
+    prods,
+    back,
+    un,
+    land,
+    s1,
+    r1,
+    s2,
+    r2a,
+    r2b,
+    so,
+    ro,
+    s3,
+    r3,
+    s4,
+    r4,
 ):
     nq = 2 * nz
     row, col = lax.axis_index("row"), lax.axis_index("col")
@@ -61,7 +105,94 @@
         return 0
 
     lax.fori_loop(1, nz, greet_line, 0)
-    pl.semaphore_wait(barrier, 2 * nq - 1 + nz - 1)
+
+    channels = nq * nz
+    ti, tj, cz = pair.shape
+
+    turned = w_in[...].astype(F32).T.astype(BF16)
+    column = jnp.broadcast_to(b_in[...], (LANES, 4 * channels)).T
+    for arr in range(2):
+        wt[arr] = turned[2 * arr * channels : 2 * (arr + 1) * channels]
+        bias[arr] = column[2 * arr * channels : 2 * (arr + 1) * channels]
+    nrm[:, tj:, :] = jnp.zeros((ti, LANES - tj, cz), BF16)
+
+    def front(arr, m):
+        def step(q, _):
+            i0 = m * ci + 4 * q
+            if arr == 1:
+                x = pair[pl.ds(i0, 4)].astype(F32)
+                centred = x - jnp.mean(x, axis=-1, keepdims=True)
+                var = jnp.mean(centred * centred, axis=-1, keepdims=True)
+                y = centred * lax.rsqrt(var + 1e-05) * norm_gain[...].reshape(1, 1, cz)
+                nrm[pl.ds(i0, 4), 0:tj, :] = y.astype(BF16)
+            rhs = nrm[pl.ds(i0, 4)].reshape(4 * LANES, cz)
+            res = lax.dot_general(
+                wt[arr], rhs, (((1,), (1,)), ((), ())), preferred_element_type=F32
+            )
+            for t in range(4):
+                value = res[0:channels, t * LANES : (t + 1) * LANES] + bias[arr, 0:channels]
+                gating = res[channels:, t * LANES : (t + 1) * LANES] + bias[arr, channels:]
+                flip[pl.ds(4 * q + t, channels, stride=ci), :] = (
+                    mask[pl.ds(i0 + t, 1), :] * sigmoid(gating) * value
+                )
+            return 0
+
+        lax.fori_loop(0, ci // 4, step, 0)
+
+        def pack(p, _):
+            for ch in range(nz):
+                ab[arr, m, p, ch] = flip[
+                    pl.ds(pl.multiple_of((p * nz + ch) * ci, ci), ci), :
+                ].astype(BF16)
+            return 0
+
+        lax.fori_loop(0, nq, pack, 0)
+
+    def gates(q, _):
+        rows = nrm[pl.ds(4 * q, 4)].reshape(4 * LANES, cz)
+        res = jnp.dot(rows, w_gate[...], preferred_element_type=F32) + b_gate[...]
+        gate[pl.ds(4 * q, 4)] = sigmoid(res).reshape(4, LANES, cz)[:, 0:tj]
+        return 0
+
+    def finish(m):
+        wait_all(land.at[m], r4.at[m])
+
+        def add(p, total):
+            for ch in range(nz):
+                total = total + land[m, p, ch].astype(F32)
+            return total
+
+        zero = jnp.zeros((ci, LANES), F32)
+        mean = lax.fori_loop(0, nq, add, zero) * (1.0 / channels)
+
+        def add_square(p, total):
+            for ch in range(nz):
+                centred = land[m, p, ch].astype(F32) - mean
+                total = total + centred * centred
+            return total
+
+        var = lax.fori_loop(0, nq, add_square, zero) * (1.0 / channels)
+        scale = lax.rsqrt(var + 1e-05)
+
+        def scaled(p, _):
+            for ch in range(nz):
+                c = p * nz + ch
+                flip[pl.ds(pl.multiple_of(c * ci, ci), ci), :] = (
+                    (land[m, p, ch].astype(F32) - mean) * scale * out_gain[0, c]
+                )
+            return 0
+
+        lax.fori_loop(0, nq, scaled, 0)
+
+        def emit(i, _):
+            normal = flip[pl.ds(i, channels, stride=ci), :].astype(BF16)
+            linear = lax.dot_general(
+                normal, w_out[...], (((0,), (0,)), ((), ())), preferred_element_type=F32
+            )
+            update[m * ci + i] = ((linear[0:tj] + b_out[...]) * gate[m * ci + i]).astype(BF16)
+            return 0
+
+        lax.fori_loop(0, ci, emit, 0)
 
     def send1(arr, m):
         def step(t, _):
@@ -124,15 +255,19 @@
         lax.fori_loop(0, nz, step, 0)
 
     order = [(1, m) for m in range(nch)] + [(0, m) for m in range(nch)]
+    front(*order[0])
+    pl.semaphore_wait(barrier, 2 * nq - 1 + nz - 1)
     send1(*order[0])
+    front(*order[1])
     send1(*order[1])
     for n, (arr, m) in enumerate(order):
         wait_all(recv1.at[arr, m], r1.at[arr, m])
+        join_and_send(arr, m)
         if n + 2 < len(order):
+            front(*order[n + 2])
             send1(*order[n + 2])
-        join_and_send(arr, m)
-
-    ti = nch * ci
+
+    lax.fori_loop(0, ti // 4, gates, 0)
     wait_all(zb, r2b)
 
     def multiply(lhs_ref, m, h):
@@ -187,13 +322,13 @@
 
             @pl.when(p == mine)
             def _():
-                pltpu.make_async_copy(un.at[m, p], out.at[m, mine], r4.at[m]).start()
+                pltpu.make_async_copy(un.at[m, p], land.at[m, mine], r4.at[m]).start()
 
             @pl.when(p != mine)
             def _():
                 pltpu.make_async_remote_copy(
                     src_ref=un.at[m, p],
-                    dst_ref=out.at[m, mine],
+                    dst_ref=land.at[m, mine],
                     send_sem=s4,
                     recv_sem=r4.at[m],
                     device_id=(2 * z + p // nz, 2 * (p % nz) + core),
@@ -213,9 +348,11 @@
         send_products(m)
         if m:
             split_and_send(m - 1)
+        if m > 1:
+            finish(m - 2)
     split_and_send(nch - 1)
-    for m in range(nch):
-        wait_all(out.at[m], r4.at[m])
+    finish(nch - 2)
+    finish(nch - 1)
 
     for arr in range(2):
         for m in range(nch):
@@ -235,18 +372,33 @@
         wait_all(un.at[m, 0 : nq - 1], s4)
 
 
-def exchange(ab, nz):
-    _, nch, nq, _, ci, _ = ab.shape
-    ti = nch * ci
+def local(pair, residue_mask, norm_gain, w_in, b_in, w_gate, b_gate, out_gain, w_out, b_out):
+    ti, tj, cz = pair.shape
+    channels = w_in.shape[1] // 4
+    nz = lax.axis_size("row") // 2
+    nq = 2 * nz
+    ci = CHUNK
+    nch = ti // ci
     depth = nq * ti
+    valid = residue_mask.astype(F32)
+    row_mask = lax.dynamic_slice_in_dim(valid, lax.axis_index("row") * ti, ti)
+    col_mask = lax.dynamic_slice_in_dim(valid, lax.axis_index("col") * tj, tj)
+    mask = row_mask[:, None] * jnp.pad(col_mask, (0, LANES - tj))[None, :]
     sem = pltpu.SemaphoreType.DMA
     vmem = pl.BlockSpec(memory_space=pltpu.VMEM)
+    smem = pl.BlockSpec(memory_space=pltpu.SMEM)
     return pl.pallas_call(
         functools.partial(triangle_kernel, nz, nch, ci),
-        out_shape=jax.ShapeDtypeStruct((nch, nq, nz, ci, LANES), BF16),
-        in_specs=[vmem],
+        out_shape=jax.ShapeDtypeStruct((ti, tj, cz), BF16),
+        in_specs=[vmem] * 7 + [smem] + [vmem] * 2,
         out_specs=vmem,
         scratch_shapes=[
+            pltpu.VMEM((ti, LANES, cz), BF16),
+            pltpu.VMEM((2, 2 * channels, cz), BF16),
+            pltpu.VMEM((2, 2 * channels, LANES), F32),
+            pltpu.VMEM((ti, tj, cz), F32),
+            pltpu.VMEM((channels * ci, LANES), F32),
+            pltpu.VMEM((2, nch, nq, nz, ci, LANES), BF16),
             pltpu.VMEM((2, nch, nq, nz, ci, LANES), BF16),
             pltpu.VMEM((2, nch, nz, ci, depth), BF16),
             pltpu.VMEM((nch, nz, ci, depth), BF16),
@@ -254,6 +406,7 @@
             pltpu.VMEM((nch, nz, ci, depth), BF16),
             pltpu.VMEM((nch, nz, 2, nz // 4, ci, 4 * ti), BF16),
             pltpu.VMEM((nch, nz, 2, nz // 4, ci, 4 * ti), BF16),
+            pltpu.VMEM((nch, nq, nz, ci, LANES), BF16),
             pltpu.VMEM((nch, nq, nz, ci, LANES), BF16),
             sem,
             sem((2, nch)),
@@ -268,48 +421,20 @@
             sem((nch,)),
         ],
         compiler_params=pltpu.CompilerParams(
-            collective_id=0, has_side_effects=True, vmem_limit_bytes=56 * 2**20
+            collective_id=0, has_side_effects=True, vmem_limit_bytes=60 * 2**20
         ),
-    )(ab)
-
-
-def local(pair, residue_mask, norm_gain, w_in, b_in, w_gate, b_gate, out_gain, w_out, b_out):
-    ti, tj, _ = pair.shape
-    channels = w_in.shape[1] // 4
-    nz = lax.axis_size("row") // 2
-    nq = 2 * nz
-    ci = 32
-    nch = ti // ci
-    row_index = lax.axis_index("row")
-    col_index = lax.axis_index("col")
-    valid = residue_mask.astype(F32)
-    row_mask = lax.dynamic_slice_in_dim(valid, row_index * ti, ti)
-    col_mask = lax.dynamic_slice_in_dim(valid, col_index * tj, tj)
-    source = pair.astype(F32)
-    mean = jnp.mean(source, axis=-1, keepdims=True)
-    centred = source - mean
-    var = jnp.mean(centred * centred, axis=-1, keepdims=True)
-    normed = (centred * lax.rsqrt(var + 1e-05) * norm_gain).astype(BF16)
-    proj = (
-        jnp.einsum("ijd,de->eij", normed, w_in, preferred_element_type=F32) + b_in[:, None, None]
+    )(
+        pair,
+        mask,
+        norm_gain.reshape(1, cz),
+        w_in,
+        b_in.reshape(1, 4 * channels),
+        w_gate,
+        b_gate.reshape(1, cz),
+        out_gain.reshape(1, channels),
+        w_out,
+        b_out.reshape(1, cz),
     )
-    masked = row_mask[:, None] * col_mask[None, :]
-    a_tile = masked * jax.nn.sigmoid(proj[channels : 2 * channels]) * proj[:channels]
-    b_tile = masked * jax.nn.sigmoid(proj[3 * channels :]) * proj[2 * channels : 3 * channels]
-    ab = jnp.stack([a_tile, b_tile]).astype(BF16)
-    ab = jnp.pad(ab, ((0, 0), (0, 0), (0, 0), (0, LANES - tj)))
-    ab = ab.reshape(2, nq, nz, nch, ci, LANES).transpose(0, 3, 1, 2, 4, 5)
-    moved = exchange(ab, nz)
-    prod = moved.transpose(1, 2, 0, 3, 4).reshape(channels, ti, LANES)[:, :, :tj].astype(F32)
-    prod_mean = jnp.mean(prod, axis=0, keepdims=True)
-    prod_centred = prod - prod_mean
-    prod_var = jnp.mean(prod_centred * prod_centred, axis=0, keepdims=True)
-    prod_norm = (prod_centred * lax.rsqrt(prod_var + 1e-05) * out_gain[:, None, None]).astype(BF16)
-    linear = jnp.einsum("cij,ce->ije", prod_norm, w_out, preferred_element_type=F32) + b_out
-    gating = jax.nn.sigmoid(
-        jnp.einsum("ijd,de->ije", normed, w_gate, preferred_element_type=F32) + b_gate
-    )
-    return (gating * linear).astype(BF16)
 
 
 def solution(mesh):

time: 246 us -> 214 us (0.87)
  local copies, waits for them, and re-layouts: 19.5 us -> 3.31 us
  other arithmetic: 16.1 us -> 1.4 us
  matrix products: 9.61 us -> 0 us
  Pallas kernels: 200 us -> 209 us
    dot_general x3 -> x0, matrix products: 9.61 us -> none  [the longest x1 5.52 us: local(): jnp.einsum('ijd,de->ije', normed, w_gate, preferred_element_type=F32)]
    pallas_call x1, Pallas kernels: 200 us -> 209 us  [local(): pl.pallas_call(functools.partial(triangle_kernel, nz, nch, ci), out_shape...]
    reduce_sum x4 -> x0, other arithmetic: 8.67 us -> none  [the longest x1 4.35 us: local(): var = jnp.mean(centred * centred, axis=-1, keepdims=True)]
    another operation x2 -> x0, other arithmetic: 5.46 us -> none  [local(): ab = jnp.stack([a_tile, b_tile]).astype(BF16)]
    unnamed x19 -> x1, local copies, waits for them, and re-layouts: 8.45 us -> 3.22 us
    reshape x1 -> x0, local copies, waits for them, and re-layouts: 4.55 us -> none  [local(): ab = ab.reshape(2, nq, nz, nch, ci, LANES).transpose(0, 3, 1, 2, 4, 5)]
    pad x1, local copies, waits for them, and re-layouts: 4 us -> 0.01 us  [local(): mask = row_mask[:, None] * jnp.pad(col_mask, (0, LANES - tj))[None, :]]
where the time goes in v2:
time: 214 us; the launch traced here: 213 us
  Pallas kernels  209 us (98%)
  local copies, waits for them, and re-layouts  3.31 us (2%)
    pallas_call x1, Pallas kernels, local(): pl.pallas_call(functools.partial(triangle_kernel, nz, nch, ci), out_shape...  209 us

profile of v2, /device:TPU:1, one launch (start us, length us, event | category | flops | bytes accessed | tf_op | source)
XLA Modules:
  0.0 213.2 jit_solution(14085783155081678517)
XLA Ops:
  0.0 0.7 convert_element_type.5
  0.7 0.1 fusion
  0.8 0.7 broadcast_multiply_fusion.mask
  1.5 208.5 %shard_map.100 = bf16[96,96,128]{2,1,0:T(8,128)(2,1)} custom-call(bf16[96,96,128]{2,1,0:T(8,128)(2,1)} %pair.1, f32[96,128]{1,0:T(8,128)} %broadcast_multiply_fusion.mask, f32[1,128]{1,0:T(1,128)} %bitcast.6, bf16[128,512]{1,0:T(8,128)(2,1)} %w_in.1, f32[1,512]{1,0:T(1,128)} %bitcast.5, bf16[128,128]{1,0:T(8,128)(2,1)} %w_gate.1, f32[1,128]{1,0:T(1,128)} %bitcast.7, ...), custom_call_target="tpu_custom_call" | custom-call | tf_op jit(solution)/shard_map/pallas_call | solution.py:390
  210.0 3.2 %copy.12 = bf16[96,96,128]{2,1,0:T(8,128)(2,1)} copy(bf16[96,96,128]{2,1,0:T(8,128)(2,1)} %shard_map.100) | data formatting | bytes 4718592
  (1 shorter events, 0.0 us)

commit v3 on v2

v3 whole, which is shorter than its diff:
```python
import functools

import jax
import jax.numpy as jnp
from jax import lax
from jax.experimental import pallas as pl
from jax.experimental.pallas import tpu as pltpu
from jax.sharding import PartitionSpec as P

MESH = pl.DeviceIdType.MESH
BF16 = jnp.bfloat16
F32 = jnp.float32
LANES = 128
CHUNK = 16
SITES = 4


def sigmoid(x):
    return 0.5 * jnp.tanh(0.5 * x) + 0.5


def join4(parts):
    lane = lax.broadcasted_iota(jnp.int32, parts[0].shape, 1)
    one, two, three = (pltpu.roll(parts[n], 128 - 32 * n, 1) for n in (1, 2, 3))
    return (
        jnp.where(lane < 96, parts[0], one),
        jnp.where(lane < 64, one, two),
        jnp.where(lane < 32, two, three),
    )


def turn8(parts):
    slot = lax.broadcasted_iota(jnp.int32, parts[0].shape, 1) // 16
    for step in (1, 2, 4):
        low = (slot // step) % 2 == 0
        turned = list(parts)
        for i in range(8):
            if not i & step:
                first, second = parts[i], parts[i | step]
                turned[i] = jnp.where(low, first, pltpu.roll(second, 16 * step, 1))
                turned[i | step] = jnp.where(low, pltpu.roll(first, 128 - 16 * step, 1), second)
        parts = turned
    return parts


def over_slots(x):
    for step in (16, 32, 64):
        x = x + pltpu.roll(x, step, 1)
    return x


def triangle_kernel(
    nz,
    pair,
    mask,
    norm_gain,
    w_in,
    b_in,
    w_gate,
    b_gate,
    out_gain,
    w_out,
    b_out,
    update,
    nrm,
    wt,
    bias,
    gate,
    flip,
    flop,
    ab,
    recv1,
    zs,
    za,
    zb,
    prods,
    back,
    un,
    land,
    s1,
    r1,
    s2,
    r2a,
    r2b,
    sf,
    rf,
    so,
    ro,
    s3,
    r3,
    s4,
    r4,
):
    nq = 2 * nz
    ci = CHUNK
    channels = nq * nz
    ti, tj, cz = pair.shape
    nch = ti // ci
    row, col = lax.axis_index("row"), lax.axis_index("col")
    z, yl = row // 2, row % 2
    w, core = col // 2, col % 2
    mine = yl * nz + w

    ahead = (nz - SITES) // 2
    site_of = [min(max(place - ahead, 0), SITES - 1) for place in range(nz)]
    group = [(site_of.index(e), site_of.index(e) + site_of.count(e)) for e in range(SITES)]
    shift = [site_of[place] - place + ahead for place in range(nz)]
    n_remote = sum(1 for d in shift if d)

    def along(d):
        return (2 * lax.rem(z + (d + nz) % nz, nz) + yl, col)

    barrier = pltpu.get_barrier_semaphore()

    def greet_plane(t, _):
        dev = lax.rem(yl * nq + col + t, 2 * nq)
        pl.semaphore_signal(
            barrier, inc=1, device_id=(2 * z + dev // nq, dev % nq), device_id_type=MESH
        )
        return 0

    lax.fori_loop(1, 2 * nq, greet_plane, 0)
    for d in range(1, ahead + 1):
        for sign in (1, -1):
            pl.semaphore_signal(barrier, inc=1, device_id=along(sign * d), device_id_type=MESH)

    turned = w_in[...].astype(F32).T.astype(BF16)
    column = jnp.broadcast_to(b_in[...], (LANES, 4 * channels)).T
    for arr in range(2):
        wt[arr] = turned[2 * arr * channels : 2 * (arr + 1) * channels]
        bias[arr] = column[2 * arr * channels : 2 * (arr + 1) * channels]
    nrm[:, tj:, :] = jnp.zeros((ti, LANES - tj, cz), BF16)
    normed = set()

    def front(arr, m):
        fresh = m not in normed
        normed.add(m)

        def step(q, _):
            i0 = m * ci + 4 * q
            if fresh:
                x = pair[pl.ds(i0, 4)].astype(F32)
                centred = x - jnp.mean(x, axis=-1, keepdims=True)
                var = jnp.mean(centred * centred, axis=-1, keepdims=True)
                y = centred * lax.rsqrt(var + 1e-05) * norm_gain[...].reshape(1, 1, cz)
                nrm[pl.ds(i0, 4), 0:tj, :] = y.astype(BF16)
            rhs = nrm[pl.ds(i0, 4)].reshape(4 * LANES, cz)
            res = lax.dot_general(
                wt[arr], rhs, (((1,), (1,)), ((), ())), preferred_element_type=F32
            )
            for t in range(4):
                value = res[0:channels, t * LANES : (t + 1) * LANES] + bias[arr, 0:channels]
                gating = res[channels:, t * LANES : (t + 1) * LANES] + bias[arr, channels:]
                flip[pl.ds(4 * q + t, channels, stride=ci), :] = (
                    mask[pl.ds(i0 + t, 1), :] * sigmoid(gating) * value
                )
            return 0

        lax.fori_loop(0, ci // 4, step, 0)

        def pack(p, _):
            for ch in range(nz):
                ab[arr, m, p, ch] = flip[
                    pl.ds(pl.multiple_of((p * nz + ch) * ci, ci), ci), :
                ].astype(BF16)
            return 0

        lax.fori_loop(0, nq, pack, 0)

    def gates(q, _):
        rows = nrm[pl.ds(4 * q, 4)].reshape(4 * LANES, cz)
        res = jnp.dot(rows, w_gate[...], preferred_element_type=F32) + b_gate[...]
        gate[pl.ds(4 * q, 4)] = sigmoid(res).reshape(4, LANES, cz)[:, 0:tj]
        return 0

    def wait_all(ref, sem):
        pltpu.make_async_copy(ref, ref, sem).wait()

    def send(src, dst, send_sem, recv_sem, device):
        pltpu.make_async_remote_copy(
            src_ref=src,
            dst_ref=dst,
            send_sem=send_sem,
            recv_sem=recv_sem,
            device_id=device,
            device_id_type=MESH,
        ).start()

    def send1(arr, m):
        def step(t, _):
            p = lax.rem(mine + t, nq)
            here = jnp.logical_and(p == mine, core == yl)

            @pl.when(here)
            def _():
                pltpu.make_async_copy(ab.at[arr, m, p], recv1.at[arr, m, col], r1.at[arr, m]).start()

            @pl.when(jnp.logical_not(here))
            def _():
                send(
                    ab.at[arr, m, p],
                    recv1.at[arr, m, col],
                    s1,
                    r1.at[arr, m],
                    (2 * z + p // nz, 2 * (p % nz) + yl),
                )

            return 0

        lax.fori_loop(0, nq, step, 0)

    def enter(arr, m):
        wait_all(recv1.at[arr, m], r1.at[arr, m])

        def step(place, _):
            ch = lax.rem(z - place + ahead + nz, nz)
            for g in range(nq // 4):
                blocks = join4([recv1[arr, m, 4 * g + n, ch].astype(F32) for n in range(4)])
                for n in range(3):
                    zs[arr, m, place, :, (3 * g + n) * LANES : (3 * g + n + 1) * LANES] = blocks[
                        n
                    ].astype(BF16)
            return 0

        lax.fori_loop(0, nz, step, 0)
        for place in sorted(range(nz), key=lambda n: -abs(shift[n])):
            if arr == 0:
                dst = za.at[core, place, m * ci : (m + 1) * ci]
                sem = r2a.at[m]
            else:
                dst = zb.at[site_of[place], m, place]
                sem = r2b.at[m, site_of[place]]
            if shift[place]:
                send(zs.at[arr, m, place], dst, s2, sem, along(shift[place]))
            else:
                pltpu.make_async_copy(zs.at[arr, m, place], dst, sem).start()

    def held(site, m, e):
        return zb.at[site, m, group[e][0] : group[e][1]]

    passed = []

    def pass_on(m, s):
        for site in range(SITES):
            if s == 1:
                wait_all(held(site, m, site), r2b.at[m, site])
            for way, e, to in ((0, site - s + 1, site + 1), (1, site + s - 1, site - 1)):
                if 0 <= e < SITES and 0 <= to < SITES:
                    if s > 1:
                        wait_all(held(site, m, e), rf.at[m, s - 1, site, way])
                    send(
                        held(site, m, e),
                        held(to, m, e),
                        sf,
                        rf.at[m, s, to, way],
                        along(to - site),
                    )
                    passed.append((site, m, e))

    def swap(m):
        part = za.at[core, :, m * ci : (m + 1) * ci]
        return pltpu.make_async_remote_copy(
            src_ref=part,
            dst_ref=part,
            send_sem=so.at[m],
            recv_sem=ro.at[m],
            device_id=(row, 2 * w + 1 - core),
            device_id_type=MESH,
        )

    def product(m):
        for s in range(1, SITES):
            wait_all(held(SITES - 1, m, SITES - 1 - s), rf.at[m, s, SITES - 1, 0])
            wait_all(held(0, m, s), rf.at[m, s, 0, 1])
        for site in range(SITES):
            first, last = group[site]

            def step(h, _):
                lhs = za[h, first:last].reshape((last - first) * ti, za.shape[-1])
                rhs = zb[site, m].reshape(nz * ci, zb.shape[-1])
                res = lax.dot_general(
                    lhs, rhs, (((1,), (1,)), ((), ())), preferred_element_type=F32
                )
                prods[m, first:last, h] = res.reshape(last - first, ti, nz * ci).astype(BF16)
                return 0

            lax.fori_loop(0, 2, step, 0)
        for place in sorted(range(nz), key=lambda n: -abs(shift[n])):
            dst = back.at[m, lax.rem(z - site_of[place] + nz, nz)]
            if shift[place]:
                send(prods.at[m, place], dst, s3, r3.at[m], along(-shift[place]))
            else:
                pltpu.make_async_copy(prods.at[m, place], dst, r3.at[m]).start()

    def turn_and_send(m):
        wait_all(back.at[m], r3.at[m])

        def step(n, _):
            h, rows = n // (ti // 16), pl.ds(pl.multiple_of(n % (ti // 16) * 16, 16), 16)
            blocks = [
                pltpu.roll(back[m, ch, h, rows].astype(F32), 16 * ((ch - ahead) % 8), 1)
                if ch != ahead
                else back[m, ch, h, rows].astype(F32)
                for ch in range(nz)
            ]
            for n, block in enumerate(turn8(blocks)):
                un[m, h * nz + n, rows] = block.astype(BF16)
            return 0

        lax.fori_loop(0, 2 * (ti // 16), step, 0)

        def go(t, _):
            p = lax.rem(mine + 1 + t, nq)

            @pl.when(p == mine)
            def _():
                pltpu.make_async_copy(un.at[m, p], land.at[m, mine], r4.at[m]).start()

            @pl.when(p != mine)
            def _():
                send(
                    un.at[m, p],
                    land.at[m, mine],
                    s4,
                    r4.at[m],
                    (2 * z + p // nz, 2 * (p % nz) + core),
                )

            return 0

        lax.fori_loop(0, nq, go, 0)

    def finish(m):
        wait_all(land.at[m], r4.at[m])
        zero = jnp.zeros((ti, LANES), F32)

        def add(p, total):
            return total + land[m, p].astype(F32)

        mean = over_slots(lax.fori_loop(0, nq, add, zero)) * (1.0 / channels)

        def add_square(p, total):
            centred = land[m, p].astype(F32) - mean
            return total + centred * centred

        var = over_slots(lax.fori_loop(0, nq, add_square, zero)) * (1.0 / channels)
        scale = lax.rsqrt(var + 1e-05)

        def scaled(p, _):
            y = (land[m, p].astype(F32) - mean) * scale * out_gain[pl.ds(p, 1), :]
            y = jnp.concatenate([y, jnp.zeros((LANES - ti, LANES), F32)], axis=0)
            flip[pl.ds(pl.multiple_of(p * LANES, LANES), LANES), :] = y.T
            return 0

        lax.fori_loop(0, nq, scaled, 0)

        def mix(j, _):
            normal = flip[pl.ds(j, channels, stride=ci), :].astype(BF16)
            linear = lax.dot_general(
                normal, w_out[...], (((0,), (0,)), ((), ())), preferred_element_type=F32
            )
            flop[pl.ds(j, ti, stride=ci), :] = linear[0:ti]
            return 0

        lax.fori_loop(0, ci, mix, 0)

        def emit(i, _):
            linear = flop[pl.ds(pl.multiple_of(i * ci, ci), ci), :] + b_out[...]
            columns = slice(m * ci, (m + 1) * ci)
            update[i, columns, :] = (linear * gate[i, columns, :]).astype(BF16)
            return 0

        lax.fori_loop(0, ti, emit, 0)

    order, b_next, a_next = [], 0, 0
    while b_next < nch:
        order.append((1, b_next))
        b_next += 1
        for _ in range(2):
            if a_next < nch:
                order.append((0, a_next))
                a_next += 1

    front(*order[0])
    pl.semaphore_wait(barrier, 2 * nq - 1 + 2 * ahead)
    send1(*order[0])
    front(*order[1])
    send1(*order[1])

    def later(k):
        for s in range(1, SITES):
            if 0 <= k - s < nch:
                pass_on(k - s, s)
        if k == SITES:
            for m in range(nch):
                swap(m).wait_recv()
        if 0 <= k - SITES < nch:
            product(k - SITES)
        if 0 <= k - SITES - 1 < nch:
            turn_and_send(k - SITES - 1)
        if 0 <= k - SITES - 2 < nch:
            finish(k - SITES - 2)

    for n, (arr, m) in enumerate(order):
        enter(arr, m)
        if n + 2 < len(order):
            front(*order[n + 2])
            send1(*order[n + 2])
        if arr == 1:
            later(m)
        elif m:
            wait_all(za.at[core, :, (m - 1) * ci : m * ci], r2a.at[m - 1])
            swap(m - 1).start()
        if (arr, m) == (0, nch - 1):
            lax.fori_loop(0, ti // 4, gates, 0)
            wait_all(za.at[core, :, m * ci :], r2a.at[m])
            swap(m).start()
    for k in range(nch, nch + SITES + 2):
        later(k)

    for arr in range(2):
        for m in range(nch):

            @pl.when(core == yl)
            def _():
                wait_all(ab.at[arr, m, 0 : nq - 1], s1)

            @pl.when(core != yl)
            def _():
                wait_all(ab.at[arr, m], s1)

            wait_all(zs.at[arr, m, 0:n_remote], s2)
    for site, m, e in passed:
        wait_all(held(site, m, e), sf)
    for m in range(nch):
        swap(m).wait_send()
        wait_all(prods.at[m, 0:n_remote], s3)
        wait_all(un.at[m, 0 : nq - 1], s4)


def local(pair, residue_mask, norm_gain, w_in, b_in, w_gate, b_gate, out_gain, w_out, b_out):
    ti, tj, cz = pair.shape
    channels = w_in.shape[1] // 4
    nz = lax.axis_size("row") // 2
    nq = 2 * nz
    ci = CHUNK
    nch = ti // ci
    depth = nq * ti
    valid = residue_mask.astype(F32)
    row_mask = lax.dynamic_slice_in_dim(valid, lax.axis_index("row") * ti, ti)
    col_mask = lax.dynamic_slice_in_dim(valid, lax.axis_index("col") * tj, tj)
    mask = row_mask[:, None] * jnp.pad(col_mask, (0, LANES - tj))[None, :]
    sem = pltpu.SemaphoreType.DMA
    vmem = pl.BlockSpec(memory_space=pltpu.VMEM)
    return pl.pallas_call(
        functools.partial(triangle_kernel, nz),
        out_shape=jax.ShapeDtypeStruct((ti, tj, cz), BF16),
        in_specs=[vmem] * 10,
        out_specs=vmem,
        scratch_shapes=[
            pltpu.VMEM((ti, LANES, cz), BF16),
            pltpu.VMEM((2, 2 * channels, cz), BF16),
            pltpu.VMEM((2, 2 * channels, LANES), F32),
            pltpu.VMEM((ti, tj, cz), F32),
            pltpu.VMEM((channels * ci, LANES), F32),
            pltpu.VMEM((ti * ci, cz), F32),
            pltpu.VMEM((2, nch, nq, nz, ci, LANES), BF16),
            pltpu.VMEM((2, nch, nq, nz, ci, LANES), BF16),
            pltpu.VMEM((2, nch, nz, ci, depth), BF16),
            pltpu.VMEM((2, nz, ti, depth), BF16),
            pltpu.VMEM((SITES, nch, nz, ci, depth), BF16),
            pltpu.VMEM((nch, nz, 2, ti, nz * ci), BF16),
            pltpu.VMEM((nch, nz, 2, ti, nz * ci), BF16),
            pltpu.VMEM((nch, nq, ti, LANES), BF16),
            pltpu.VMEM((nch, nq, ti, LANES), BF16),
            sem,
            sem((2, nch)),
            sem,
            sem((nch,)),
            sem((nch, SITES)),
            sem,
            sem((nch, SITES, SITES, 2)),
            sem((nch,)),
            sem((nch,)),
            sem,
            sem((nch,)),
            sem,
            sem((nch,)),
        ],
        compiler_params=pltpu.CompilerParams(
            collective_id=0, has_side_effects=True, vmem_limit_bytes=60 * 2**20
        ),
    )(
        pair,
        mask,
        norm_gain.reshape(1, cz),
        w_in,
        b_in.reshape(1, 4 * channels),
        w_gate,
        b_gate.reshape(1, cz),
        jnp.repeat(out_gain, ci).reshape(nq, LANES),
        w_out,
        b_out.reshape(1, cz),
    )


def solution(mesh):
    in_specs = (P("row", "col", None), P(), P(), P(), P(), P(), P(), P(), P(), P())
    out_specs = P("row", "col", None)
    return jax.shard_map(local, mesh=mesh, in_specs=in_specs, out_specs=out_specs, check_vma=False)
```

time: 214 us -> 222 us (1.037)
  Pallas kernels: 209 us -> 216 us
    pallas_call x1, Pallas kernels: 209 us -> 216 us  [local(): pl.pallas_call(functools.partial(triangle_kernel, nz), out_shape=jax.Shap...]
where the time goes in v3:
time: 222 us
  Pallas kernels  216 us (97%)
  local copies, waits for them, and re-layouts  4.79 us (2%)
    pallas_call x1, Pallas kernels, local(): pl.pallas_call(functools.partial(triangle_kernel, nz), out_shape=jax.Shap...  216 us

profile of v3, /device:TPU:1, one launch (start us, length us, event | category | flops | bytes accessed | tf_op | source)
XLA Modules:
  0.0 222.0 jit_solution(4345237624824170855)
XLA Ops:
  0.0 0.7 convert_element_type.5
  0.7 0.1 fusion
  0.8 0.7 broadcast_in_dim.9
  1.5 0.7 broadcast_multiply_fusion.mask
  2.2 0.1 broadcast_in_dim.10
  2.3 0.7 broadcast_in_dim.11.out_gain
  3.0 215.7 %shard_map.100 = bf16[96,96,128]{2,1,0:T(8,128)(2,1)} custom-call(bf16[96,96,128]{2,1,0:T(8,128)(2,1)} %pair.1, f32[96,128]{1,0:T(8,128)} %broadcast_multiply_fusion.mask, f32[1,128]{1,0:T(1,128)} %bitcast.5, bf16[128,512]{1,0:T(8,128)(2,1)} %w_in.1, f32[1,512]{1,0:T(1,128)} %bitcast.4, bf16[128,128]{1,0:T(8,128)(2,1)} %w_gate.1, f32[1,128]{1,0:T(1,128)} %bitcast.6, ...), custom_call_target="tpu_custom_call" | custom-call | tf_op jit(solution)/shard_map/pallas_call | solution.py:455
  218.7 3.2 %copy.12 = bf16[96,96,128]{2,1,0:T(8,128)(2,1)} copy(bf16[96,96,128]{2,1,0:T(8,128)(2,1)} %shard_map.100) | data formatting | bytes 4718592
  (1 shorter events, 0.0 us)

commit v4 on v3

--- a/solution.py
+++ b/solution.py
@@ -12,7 +12,7 @@
 F32 = jnp.float32
 LANES = 128
 CHUNK = 16
-SITES = 4
+SITES = 2
 
 
 def sigmoid(x):
@@ -156,7 +156,7 @@
                 )
             return 0
 
-        lax.fori_loop(0, ci // 4, step, 0)
+        lax.fori_loop(0, ci // 4, step, 0, unroll=2)
 
         def pack(p, _):
             for ch in range(nz):
@@ -165,7 +165,7 @@
                 ].astype(BF16)
             return 0
 
-        lax.fori_loop(0, nq, pack, 0)
+        lax.fori_loop(0, nq, pack, 0, unroll=2)
 
     def gates(q, _):
         rows = nrm[pl.ds(4 * q, 4)].reshape(4 * LANES, cz)
@@ -225,7 +225,7 @@
         lax.fori_loop(0, nz, step, 0)
         for place in sorted(range(nz), key=lambda n: -abs(shift[n])):
             if arr == 0:
-                dst = za.at[core, place, m * ci : (m + 1) * ci]
+                dst = za.at[place, core, m * ci : (m + 1) * ci]
                 sem = r2a.at[m]
             else:
                 dst = zb.at[site_of[place], m, place]
@@ -258,7 +258,7 @@
                     passed.append((site, m, e))
 
     def swap(m):
-        part = za.at[core, :, m * ci : (m + 1) * ci]
+        part = za.at[:, core, m * ci : (m + 1) * ci]
         return pltpu.make_async_remote_copy(
             src_ref=part,
             dst_ref=part,
@@ -275,16 +275,14 @@
         for site in range(SITES):
             first, last = group[site]
 
-            def step(h, _):
-                lhs = za[h, first:last].reshape((last - first) * ti, za.shape[-1])
-                rhs = zb[site, m].reshape(nz * ci, zb.shape[-1])
-                res = lax.dot_general(
-                    lhs, rhs, (((1,), (1,)), ((), ())), preferred_element_type=F32
-                )
-                prods[m, first:last, h] = res.reshape(last - first, ti, nz * ci).astype(BF16)
-                return 0
-
-            lax.fori_loop(0, 2, step, 0)
+            rows = (last - first) * 2 * ti
+            res = lax.dot_general(
+                za[first:last].reshape(rows, za.shape[-1]),
+                zb[site, m].reshape(nz * ci, zb.shape[-1]),
+                (((1,), (1,)), ((), ())),
+                preferred_element_type=F32,
+            )
+            prods[m, first:last] = res.reshape(last - first, 2, ti, nz * ci).astype(BF16)
         for place in sorted(range(nz), key=lambda n: -abs(shift[n])):
             dst = back.at[m, lax.rem(z - site_of[place] + nz, nz)]
             if shift[place]:
@@ -296,7 +294,7 @@
         wait_all(back.at[m], r3.at[m])
 
         def step(n, _):
-            h, rows = n // (ti // 16), pl.ds(pl.multiple_of(n % (ti // 16) * 16, 16), 16)
+            h, rows = n // 3, pl.ds(pl.multiple_of(n % 3 * 32, 32), 32)
             blocks = [
                 pltpu.roll(back[m, ch, h, rows].astype(F32), 16 * ((ch - ahead) % 8), 1)
                 if ch != ahead
@@ -307,7 +305,7 @@
                 un[m, h * nz + n, rows] = block.astype(BF16)
             return 0
 
-        lax.fori_loop(0, 2 * (ti // 16), step, 0)
+        lax.fori_loop(0, 6, step, 0)
 
         def go(t, _):
             p = lax.rem(mine + 1 + t, nq)
@@ -332,19 +330,15 @@
 
     def finish(m):
         wait_all(land.at[m], r4.at[m])
-        zero = jnp.zeros((ti, LANES), F32)
-
-        def add(p, total):
-            return total + land[m, p].astype(F32)
-
-        mean = over_slots(lax.fori_loop(0, nq, add, zero)) * (1.0 / channels)
-
-        def add_square(p, total):
+        total = jnp.zeros((ti, LANES), F32)
+        for p in range(nq):
+            total = total + land[m, p].astype(F32)
+        mean = over_slots(total) * (1.0 / channels)
+        total = jnp.zeros((ti, LANES), F32)
+        for p in range(nq):
             centred = land[m, p].astype(F32) - mean
-            return total + centred * centred
-
-        var = over_slots(lax.fori_loop(0, nq, add_square, zero)) * (1.0 / channels)
-        scale = lax.rsqrt(var + 1e-05)
+            total = total + centred * centred
+        scale = lax.rsqrt(over_slots(total) * (1.0 / channels) + 1e-05)
 
         def scaled(p, _):
             y = (land[m, p].astype(F32) - mean) * scale * out_gain[pl.ds(p, 1), :]
@@ -352,7 +346,7 @@
             flip[pl.ds(pl.multiple_of(p * LANES, LANES), LANES), :] = y.T
             return 0
 
-        lax.fori_loop(0, nq, scaled, 0)
+        lax.fori_loop(0, nq, scaled, 0, unroll=4)
 
         def mix(j, _):
             normal = flip[pl.ds(j, channels, stride=ci), :].astype(BF16)
@@ -362,15 +356,17 @@
             flop[pl.ds(j, ti, stride=ci), :] = linear[0:ti]
             return 0
 
-        lax.fori_loop(0, ci, mix, 0)
-
-        def emit(i, _):
-            linear = flop[pl.ds(pl.multiple_of(i * ci, ci), ci), :] + b_out[...]
-            columns = slice(m * ci, (m + 1) * ci)
-            update[i, columns, :] = (linear * gate[i, columns, :]).astype(BF16)
-            return 0
-
-        lax.fori_loop(0, ti, emit, 0)
+        lax.fori_loop(0, ci, mix, 0, unroll=4)
+
+        def emit(n, _):
+            rows, columns = pl.ds(8 * n, 8), slice(m * ci, (m + 1) * ci)
+            linear = flop[pl.ds(pl.multiple_of(8 * n * ci, 8 * ci), 8 * ci), :] + b_out[...]
+            update[rows, columns, :] = (
+                linear.reshape(8, ci, cz) * gate[rows, columns, :]
+            ).astype(BF16)
+            return 0
+
+        lax.fori_loop(0, ti // 8, emit, 0, unroll=2)
 
     order, b_next, a_next = [], 0, 0
     while b_next < nch:
@@ -387,19 +383,25 @@
     front(*order[1])
     send1(*order[1])
 
+    done = {"product": 0, "turn": 0, "finish": 0}
+    first_product = 1 + next(m for arr, m in order[order.index((0, nch - 1)) :: -1] if arr)
+
     def later(k):
         for s in range(1, SITES):
             if 0 <= k - s < nch:
                 pass_on(k - s, s)
-        if k == SITES:
+        if k < first_product:
+            return
+        if k == first_product:
             for m in range(nch):
                 swap(m).wait_recv()
-        if 0 <= k - SITES < nch:
-            product(k - SITES)
-        if 0 <= k - SITES - 1 < nch:
-            turn_and_send(k - SITES - 1)
-        if 0 <= k - SITES - 2 < nch:
-            finish(k - SITES - 2)
+        for n, (name, act) in enumerate(
+            (("product", product), ("turn", turn_and_send), ("finish", finish))
+        ):
+            last = min(k - SITES - n, nch - 1) if k >= first_product + n else -1
+            while done[name] <= last:
+                act(done[name])
+                done[name] += 1
 
     for n, (arr, m) in enumerate(order):
         enter(arr, m)
@@ -409,11 +411,11 @@
         if arr == 1:
             later(m)
         elif m:
-            wait_all(za.at[core, :, (m - 1) * ci : m * ci], r2a.at[m - 1])
+            wait_all(za.at[:, core, (m - 1) * ci : m * ci], r2a.at[m - 1])
             swap(m - 1).start()
         if (arr, m) == (0, nch - 1):
-            lax.fori_loop(0, ti // 4, gates, 0)
-            wait_all(za.at[core, :, m * ci :], r2a.at[m])
+            lax.fori_loop(0, ti // 4, gates, 0, unroll=2)
+            wait_all(za.at[:, core, m * ci :], r2a.at[m])
             swap(m).start()
     for k in range(nch, nch + SITES + 2):
         later(k)
@@ -467,7 +469,7 @@
             pltpu.VMEM((2, nch, nq, nz, ci, LANES), BF16),
             pltpu.VMEM((2, nch, nq, nz, ci, LANES), BF16),
             pltpu.VMEM((2, nch, nz, ci, depth), BF16),
-            pltpu.VMEM((2, nz, ti, depth), BF16),
+            pltpu.VMEM((nz, 2, ti, depth), BF16),
             pltpu.VMEM((SITES, nch, nz, ci, depth), BF16),
             pltpu.VMEM((nch, nz, 2, ti, nz * ci), BF16),
             pltpu.VMEM((nch, nz, 2, ti, nz * ci), BF16),

time: 222 us -> 186 us (0.84)
  Pallas kernels: 216 us -> 180 us
    pallas_call x1, Pallas kernels: 216 us -> 180 us  [local(): pl.pallas_call(functools.partial(triangle_kernel, nz), out_shape=jax.Shap...]
where the time goes in v4:
time: 186 us
  Pallas kernels  180 us (97%)
  local copies, waits for them, and re-layouts  4.79 us (3%)
    pallas_call x1, Pallas kernels, local(): pl.pallas_call(functools.partial(triangle_kernel, nz), out_shape=jax.Shap...  180 us

profile of v4, /device:TPU:1, one launch (start us, length us, event | category | flops | bytes accessed | tf_op | source)
XLA Modules:
  0.0 186.1 jit_solution(9317828279926859084)
XLA Ops:
  0.0 0.7 convert_element_type.5
  0.7 0.1 fusion
  0.8 0.7 broadcast_in_dim.9
  1.5 0.7 broadcast_multiply_fusion.mask
  2.2 0.1 broadcast_in_dim.10
  2.3 0.7 broadcast_in_dim.11.out_gain
  3.0 179.9 %shard_map.100 = bf16[96,96,128]{2,1,0:T(8,128)(2,1)} custom-call(bf16[96,96,128]{2,1,0:T(8,128)(2,1)} %pair.1, f32[96,128]{1,0:T(8,128)} %broadcast_multiply_fusion.mask, f32[1,128]{1,0:T(1,128)} %bitcast.5, bf16[128,512]{1,0:T(8,128)(2,1)} %w_in.1, f32[1,512]{1,0:T(1,128)} %bitcast.4, bf16[128,128]{1,0:T(8,128)(2,1)} %w_gate.1, f32[1,128]{1,0:T(1,128)} %bitcast.6, ...), custom_call_target="tpu_custom_call" | custom-call | tf_op jit(solution)/shard_map/pallas_call | solution.py:457
  182.9 3.2 %copy.12 = bf16[96,96,128]{2,1,0:T(8,128)(2,1)} copy(bf16[96,96,128]{2,1,0:T(8,128)(2,1)} %shard_map.100) | data formatting | bytes 4718592
  (1 shorter events, 0.0 us)

commit v5 on v4

--- a/solution.py
+++ b/solution.py
@@ -52,13 +52,13 @@
 def triangle_kernel(
     nz,
     pair,
-    mask,
+    valid,
     norm_gain,
     w_in,
     b_in,
     w_gate,
     b_gate,
-    out_gain,
+    gain,
     w_out,
     b_out,
     update,
@@ -68,7 +68,9 @@
     gate,
     flip,
     flop,
+    out_gain,
     ab,
+    zf,
     recv1,
     zs,
     za,
@@ -79,6 +81,8 @@
     land,
     s1,
     r1,
+    sz,
+    rz,
     s2,
     r2a,
     r2b,
@@ -130,6 +134,21 @@
         wt[arr] = turned[2 * arr * channels : 2 * (arr + 1) * channels]
         bias[arr] = column[2 * arr * channels : 2 * (arr + 1) * channels]
     nrm[:, tj:, :] = jnp.zeros((ti, LANES - tj, cz), BF16)
+    lane = lax.broadcasted_iota(jnp.int32, (1, LANES), 1)
+
+    def col_valid(j, mask):
+        return jnp.where(lane == j, valid[col * tj + j].astype(F32), mask)
+
+    mask = lax.fori_loop(0, tj, col_valid, jnp.zeros((1, LANES), F32), unroll=8)
+
+    def spread(p, _):
+        line = jnp.zeros((1, LANES), F32)
+        for ch in range(nz):
+            line = jnp.where(lane // ci == ch, gain[p * nz + ch], line)
+        out_gain[pl.ds(p, 1), :] = line
+        return 0
+
+    lax.fori_loop(0, nq, spread, 0)
     normed = set()
 
     def front(arr, m):
@@ -151,8 +170,9 @@
             for t in range(4):
                 value = res[0:channels, t * LANES : (t + 1) * LANES] + bias[arr, 0:channels]
                 gating = res[channels:, t * LANES : (t + 1) * LANES] + bias[arr, channels:]
+                pair_mask = mask * valid[row * ti + i0 + t].astype(F32)
                 flip[pl.ds(4 * q + t, channels, stride=ci), :] = (
-                    mask[pl.ds(i0 + t, 1), :] * sigmoid(gating) * value
+                    pair_mask * sigmoid(gating) * value
                 )
             return 0
 
@@ -186,19 +206,21 @@
             device_id_type=MESH,
         ).start()
 
-    def send1(arr, m):
+    def send1(arr, m, src=None):
+        src = ab.at[arr, m] if src is None else src
+
         def step(t, _):
             p = lax.rem(mine + t, nq)
             here = jnp.logical_and(p == mine, core == yl)
 
             @pl.when(here)
             def _():
-                pltpu.make_async_copy(ab.at[arr, m, p], recv1.at[arr, m, col], r1.at[arr, m]).start()
+                pltpu.make_async_copy(src.at[p], recv1.at[arr, m, col], r1.at[arr, m]).start()
 
             @pl.when(jnp.logical_not(here))
             def _():
                 send(
-                    ab.at[arr, m, p],
+                    src.at[p],
                     recv1.at[arr, m, col],
                     s1,
                     r1.at[arr, m],
@@ -209,21 +231,41 @@
 
         lax.fori_loop(0, nq, step, 0)
 
+    far_first = sorted(range(nz), key=lambda place: -abs(shift[place]))
+
+    def z_first():
+        for place in far_first:
+            src = ab.at[0, 0, :, lax.rem(z - place + ahead + nz, nz)]
+            if shift[place]:
+                send(src, zf.at[:, place], sz, rz, along(shift[place]))
+            else:
+                pltpu.make_async_copy(src, zf.at[:, place], rz).start()
+
+    def then_plane():
+        wait_all(zf, rz)
+        send1(0, 0, zf)
+
     def enter(arr, m):
         wait_all(recv1.at[arr, m], r1.at[arr, m])
 
+        at_site = (arr, m) == (0, 0)
+
         def step(place, _):
-            ch = lax.rem(z - place + ahead + nz, nz)
+            block = place if at_site else lax.rem(z - place + ahead + nz, nz)
             for g in range(nq // 4):
-                blocks = join4([recv1[arr, m, 4 * g + n, ch].astype(F32) for n in range(4)])
+                joined = join4([recv1[arr, m, 4 * g + n, block].astype(F32) for n in range(4)])
                 for n in range(3):
-                    zs[arr, m, place, :, (3 * g + n) * LANES : (3 * g + n + 1) * LANES] = blocks[
-                        n
-                    ].astype(BF16)
+                    lanes = slice((3 * g + n) * LANES, (3 * g + n + 1) * LANES)
+                    if at_site:
+                        za[place, core, 0:ci, lanes] = joined[n].astype(BF16)
+                    else:
+                        zs[arr, m, place, :, lanes] = joined[n].astype(BF16)
             return 0
 
         lax.fori_loop(0, nz, step, 0)
-        for place in sorted(range(nz), key=lambda n: -abs(shift[n])):
+        if at_site:
+            return
+        for place in far_first:
             if arr == 0:
                 dst = za.at[place, core, m * ci : (m + 1) * ci]
                 sem = r2a.at[m]
@@ -283,7 +325,7 @@
                 preferred_element_type=F32,
             )
             prods[m, first:last] = res.reshape(last - first, 2, ti, nz * ci).astype(BF16)
-        for place in sorted(range(nz), key=lambda n: -abs(shift[n])):
+        for place in far_first:
             dst = back.at[m, lax.rem(z - site_of[place] + nz, nz)]
             if shift[place]:
                 send(prods.at[m, place], dst, s3, r3.at[m], along(-shift[place]))
@@ -368,57 +410,91 @@
 
         lax.fori_loop(0, ti // 8, emit, 0, unroll=2)
 
-    order, b_next, a_next = [], 0, 0
-    while b_next < nch:
-        order.append((1, b_next))
-        b_next += 1
-        for _ in range(2):
-            if a_next < nch:
-                order.append((0, a_next))
-                a_next += 1
-
-    front(*order[0])
+    def join_swap(m):
+        if m:
+            wait_all(za.at[:, core, m * ci : (m + 1) * ci], r2a.at[m])
+        swap(m).start()
+
+    def all_gates():
+        lax.fori_loop(0, ti // 4, gates, 0, unroll=2)
+
+    def all_of_a():
+        for m in range(nch):
+            swap(m).wait_recv()
+
+    first = [(0, 0), (1, 0), (0, 1), (1, 1)]
+    for chunk in first:
+        front(*chunk)
     pl.semaphore_wait(barrier, 2 * nq - 1 + 2 * ahead)
-    send1(*order[0])
-    front(*order[1])
-    send1(*order[1])
-
-    done = {"product": 0, "turn": 0, "finish": 0}
-    first_product = 1 + next(m for arr, m in order[order.index((0, nch - 1)) :: -1] if arr)
-
-    def later(k):
-        for s in range(1, SITES):
-            if 0 <= k - s < nch:
-                pass_on(k - s, s)
-        if k < first_product:
-            return
-        if k == first_product:
-            for m in range(nch):
-                swap(m).wait_recv()
-        for n, (name, act) in enumerate(
-            (("product", product), ("turn", turn_and_send), ("finish", finish))
-        ):
-            last = min(k - SITES - n, nch - 1) if k >= first_product + n else -1
-            while done[name] <= last:
-                act(done[name])
-                done[name] += 1
-
-    for n, (arr, m) in enumerate(order):
-        enter(arr, m)
-        if n + 2 < len(order):
-            front(*order[n + 2])
-            send1(*order[n + 2])
-        if arr == 1:
-            later(m)
-        elif m:
-            wait_all(za.at[:, core, (m - 1) * ci : m * ci], r2a.at[m - 1])
-            swap(m - 1).start()
-        if (arr, m) == (0, nch - 1):
-            lax.fori_loop(0, ti // 4, gates, 0, unroll=2)
-            wait_all(za.at[:, core, m * ci :], r2a.at[m])
-            swap(m).start()
-    for k in range(nch, nch + SITES + 2):
-        later(k)
+    plan = [
+        (z_first,),
+        (send1, 1, 0),
+        (send1, 0, 1),
+        (front, 0, 2),
+        (enter, 1, 0),
+        (send1, 1, 1),
+        (front, 0, 3),
+        (front, 1, 2),
+        (then_plane,),
+        (enter, 0, 1),
+        (send1, 0, 2),
+        (front, 0, 4),
+        (pass_on, 0, 1),
+        (enter, 1, 1),
+        (send1, 0, 3),
+        (front, 0, 5),
+        (enter, 0, 2),
+        (send1, 1, 2),
+        (enter, 0, 0),
+        (join_swap, 0),
+        (join_swap, 1),
+        (front, 1, 3),
+        (pass_on, 1, 1),
+        (enter, 0, 3),
+        (send1, 0, 4),
+        (front, 1, 4),
+        (join_swap, 2),
+        (all_gates,),
+        (enter, 1, 2),
+        (send1, 0, 5),
+        (front, 1, 5),
+        (enter, 0, 4),
+        (send1, 1, 3),
+        (join_swap, 3),
+        (enter, 0, 5),
+        (send1, 1, 4),
+        (pass_on, 2, 1),
+        (enter, 1, 3),
+        (send1, 1, 5),
+        (join_swap, 4),
+        (enter, 1, 4),
+        (join_swap, 5),
+        (enter, 1, 5),
+        (all_of_a,),
+        (product, 0),
+        (product, 1),
+        (pass_on, 3, 1),
+        (product, 2),
+        (pass_on, 4, 1),
+        (pass_on, 5, 1),
+        (turn_and_send, 0),
+        (turn_and_send, 1),
+        (finish, 0),
+        (turn_and_send, 2),
+        (finish, 1),
+        (product, 3),
+        (finish, 2),
+        (product, 4),
+        (product, 5),
+        (turn_and_send, 3),
+        (turn_and_send, 4),
+        (finish, 3),
+        (turn_and_send, 5),
+        (finish, 4),
+        (finish, 5),
+    ]
+    for act, *which in plan:
+        act(*which)
 
     for arr in range(2):
         for m in range(nch):
@@ -431,7 +507,9 @@
             def _():
                 wait_all(ab.at[arr, m], s1)
 
-            wait_all(zs.at[arr, m, 0:n_remote], s2)
+            if (arr, m) != (0, 0):
+                wait_all(zs.at[arr, m, 0:n_remote], s2)
+    wait_all(zf.at[:, 0:n_remote], sz)
     for site, m, e in passed:
         wait_all(held(site, m, e), sf)
     for m in range(nch):
@@ -448,16 +526,13 @@
     ci = CHUNK
     nch = ti // ci
     depth = nq * ti
-    valid = residue_mask.astype(F32)
-    row_mask = lax.dynamic_slice_in_dim(valid, lax.axis_index("row") * ti, ti)
-    col_mask = lax.dynamic_slice_in_dim(valid, lax.axis_index("col") * tj, tj)
-    mask = row_mask[:, None] * jnp.pad(col_mask, (0, LANES - tj))[None, :]
     sem = pltpu.SemaphoreType.DMA
     vmem = pl.BlockSpec(memory_space=pltpu.VMEM)
+    smem = pl.BlockSpec(memory_space=pltpu.SMEM)
     return pl.pallas_call(
         functools.partial(triangle_kernel, nz),
         out_shape=jax.ShapeDtypeStruct((ti, tj, cz), BF16),
-        in_specs=[vmem] * 10,
+        in_specs=[vmem, smem] + [vmem] * 5 + [smem] + [vmem] * 2,
         out_specs=vmem,
         scratch_shapes=[
             pltpu.VMEM((ti, LANES, cz), BF16),
@@ -466,7 +541,9 @@
             pltpu.VMEM((ti, tj, cz), F32),
             pltpu.VMEM((channels * ci, LANES), F32),
             pltpu.VMEM((ti * ci, cz), F32),
+            pltpu.VMEM((nq, LANES), F32),
             pltpu.VMEM((2, nch, nq, nz, ci, LANES), BF16),
+            pltpu.VMEM((nq, nz, ci, LANES), BF16),
             pltpu.VMEM((2, nch, nq, nz, ci, LANES), BF16),
             pltpu.VMEM((2, nch, nz, ci, depth), BF16),
             pltpu.VMEM((nz, 2, ti, depth), BF16),
@@ -478,6 +555,8 @@
             sem,
             sem((2, nch)),
             sem,
+            sem,
+            sem,
             sem((nch,)),
             sem((nch, SITES)),
             sem,
@@ -494,13 +573,13 @@
         ),
     )(
         pair,
-        mask,
+        residue_mask,
         norm_gain.reshape(1, cz),
         w_in,
         b_in.reshape(1, 4 * channels),
         w_gate,
         b_gate.reshape(1, cz),
-        jnp.repeat(out_gain, ci).reshape(nq, LANES),
+        out_gain,
         w_out,
         b_out.reshape(1, cz),
     )

time: 186 us -> 178 us (0.957)
  Pallas kernels: 180 us -> 174 us
    pallas_call x1, Pallas kernels: 180 us -> 174 us  [local(): pl.pallas_call(functools.partial(triangle_kernel, nz), out_shape=jax.Shap...]
where the time goes in v5:
time: 178 us
  Pallas kernels  174 us (98%)
  local copies, waits for them, and re-layouts  3.22 us (2%)
    pallas_call x1, Pallas kernels, local(): pl.pallas_call(functools.partial(triangle_kernel, nz), out_shape=jax.Shap...  174 us

profile of v5, /device:TPU:1, one launch (start us, length us, event | category | flops | bytes accessed | tf_op | source)
XLA Modules:
  0.0 177.7 jit_solution(7536219695304283332)
XLA Ops:
  0.0 174.4 %shard_map.100 = bf16[96,96,128]{2,1,0:T(8,128)(2,1)} custom-call(bf16[96,96,128]{2,1,0:T(8,128)(2,1)} %pair.1, s32[1536]{0:T(1024)} %valid.1, f32[1,128]{1,0:T(1,128)} %bitcast.5, bf16[128,512]{1,0:T(8,128)(2,1)} %w_in.1, f32[1,512]{1,0:T(1,128)} %bitcast.4, bf16[128,128]{1,0:T(8,128)(2,1)} %w_gate.1, f32[1,128]{1,0:T(1,128)} %bitcast.6, f32[128]{0:T(128)} %gain.1, ...), custom_call_target="tpu_custom_call" | custom-call | tf_op jit(solution)/shard_map/pallas_call | solution.py:532
  174.4 3.2 %copy.12 = bf16[96,96,128]{2,1,0:T(8,128)(2,1)} copy(bf16[96,96,128]{2,1,0:T(8,128)(2,1)} %shard_map.100) | data formatting | bytes 4718592

commit v6 on v5

--- a/solution.py
+++ b/solution.py
@@ -51,7 +51,7 @@
 
 def triangle_kernel(
     nz,
-    pair,
+    pair_in,
     valid,
     norm_gain,
     w_in,
@@ -62,6 +62,8 @@
     w_out,
     b_out,
     update,
+    pair,
+    sp,
     nrm,
     wt,
     bias,
@@ -69,6 +71,8 @@
     flip,
     flop,
     out_gain,
+    late_gain,
+    w_late,
     ab,
     zf,
     recv1,
@@ -79,6 +83,8 @@
     back,
     un,
     land,
+    mid,
+    rm,
     s1,
     r1,
     sz,
@@ -128,6 +134,9 @@
         for sign in (1, -1):
             pl.semaphore_signal(barrier, inc=1, device_id=along(sign * d), device_id_type=MESH)
 
+    load = pltpu.make_async_copy(pair_in, pair, sp)
+    load.start()
+
     turned = w_in[...].astype(F32).T.astype(BF16)
     column = jnp.broadcast_to(b_in[...], (LANES, 4 * channels)).T
     for arr in range(2):
@@ -146,9 +155,16 @@
         for ch in range(nz):
             line = jnp.where(lane // ci == ch, gain[p * nz + ch], line)
         out_gain[pl.ds(p, 1), :] = line
+        line = jnp.zeros((1, LANES), F32)
+        for n in range(nz):
+            line = jnp.where(lane // ci == n, gain[(p % 2 * nz + n) * nz + p // 2], line)
+        late_gain[pl.ds(p, 1), :] = line
         return 0
 
     lax.fori_loop(0, nq, spread, 0)
+    flop[0:channels, :] = w_out[...].astype(F32)
+    for ch in range(nz):
+        w_late[ch * nq : (ch + 1) * nq] = flop[pl.ds(ch, nq, stride=nz), :].astype(BF16)
     normed = set()
 
     def front(arr, m):
@@ -325,6 +341,10 @@
                 preferred_element_type=F32,
             )
             prods[m, first:last] = res.reshape(last - first, 2, ti, nz * ci).astype(BF16)
+        if m < nch - 1:
+            send_back(m)
+
+    def send_back(m):
         for place in far_first:
             dst = back.at[m, lax.rem(z - site_of[place] + nz, nz)]
             if shift[place]:
@@ -332,58 +352,91 @@
             else:
                 pltpu.make_async_copy(prods.at[m, place], dst, r3.at[m]).start()
 
+    def turn(m, load_block, store_block):
+        def step(n, _):
+            h, rows = n // 3, pl.ds(pl.multiple_of(n % 3 * 32, 32), 32)
+            for i, block in enumerate(turn8([load_block(i, h, rows) for i in range(nz)])):
+                store_block(i, h, rows, block.astype(BF16))
+            return 0
+
+        lax.fori_loop(0, 6, step, 0)
+
+    def to_plane(m, dst, sem):
+        def go(t, _):
+            p = lax.rem(mine + 1 + t, nq)
+
+            @pl.when(p == mine)
+            def _():
+                pltpu.make_async_copy(un.at[m, p], dst.at[mine], sem).start()
+
+            @pl.when(p != mine)
+            def _():
+                device = (2 * z + p // nz, 2 * (p % nz) + core)
+                send(un.at[m, p], dst.at[mine], s4, sem, device)
+
+            return 0
+
+        lax.fori_loop(0, nq, go, 0)
+
+    def store_un(m):
+        def store(i, h, rows, block):
+            un[m, h * nz + i, rows] = block
+
+        return store
+
     def turn_and_send(m):
         wait_all(back.at[m], r3.at[m])
 
-        def step(n, _):
-            h, rows = n // 3, pl.ds(pl.multiple_of(n % 3 * 32, 32), 32)
-            blocks = [
-                pltpu.roll(back[m, ch, h, rows].astype(F32), 16 * ((ch - ahead) % 8), 1)
-                if ch != ahead
-                else back[m, ch, h, rows].astype(F32)
-                for ch in range(nz)
-            ]
-            for n, block in enumerate(turn8(blocks)):
-                un[m, h * nz + n, rows] = block.astype(BF16)
-            return 0
-
-        lax.fori_loop(0, 6, step, 0)
-
-        def go(t, _):
-            p = lax.rem(mine + 1 + t, nq)
-
-            @pl.when(p == mine)
-            def _():
-                pltpu.make_async_copy(un.at[m, p], land.at[m, mine], r4.at[m]).start()
-
-            @pl.when(p != mine)
-            def _():
-                send(
-                    un.at[m, p],
-                    land.at[m, mine],
-                    s4,
-                    r4.at[m],
-                    (2 * z + p // nz, 2 * (p % nz) + core),
-                )
-
-            return 0
-
-        lax.fori_loop(0, nq, go, 0)
+        def load_block(ch, h, rows):
+            block = back[m, ch, h, rows].astype(F32)
+            return pltpu.roll(block, 16 * ((ch - ahead) % nz), 1) if ch != ahead else block
+
+        turn(m, load_block, store_un(m))
+        to_plane(m, land.at[m], r4.at[m])
+
+    def turn_at_site(m):
+        def load_block(place, h, rows):
+            amount = 16 * lax.rem(z - site_of[place] - ahead + 2 * nz, nz)
+            return pltpu.roll(prods[m, place, h, rows].astype(F32), amount, 1)
+
+        turn(m, load_block, store_un(m))
+        to_plane(m, mid, rm)
+
+    def turn_and_return(m):
+        wait_all(mid, rm)
+
+        def load_block(n, half, rows):
+            return mid[half * nz + n, rows].astype(F32)
+
+        def store_block(place, half, rows, block):
+            prods[m, place, half, rows] = block
+
+        turn(m, load_block, store_block)
+        send_back(m)
 
     def finish(m):
-        wait_all(land.at[m], r4.at[m])
+        late = m == nch - 1
+        if late:
+            wait_all(back.at[m], r3.at[m])
+        else:
+            wait_all(land.at[m], r4.at[m])
+        gains, weights = (late_gain, w_late) if late else (out_gain, w_out)
+
+        def block(p):
+            return (back[m, p // 2, p % 2] if late else land[m, p]).astype(F32)
+
         total = jnp.zeros((ti, LANES), F32)
         for p in range(nq):
-            total = total + land[m, p].astype(F32)
+            total = total + block(p)
         mean = over_slots(total) * (1.0 / channels)
         total = jnp.zeros((ti, LANES), F32)
         for p in range(nq):
-            centred = land[m, p].astype(F32) - mean
+            centred = block(p) - mean
             total = total + centred * centred
         scale = lax.rsqrt(over_slots(total) * (1.0 / channels) + 1e-05)
 
         def scaled(p, _):
-            y = (land[m, p].astype(F32) - mean) * scale * out_gain[pl.ds(p, 1), :]
+            y = (block(p) - mean) * scale * gains[pl.ds(p, 1), :]
             y = jnp.concatenate([y, jnp.zeros((LANES - ti, LANES), F32)], axis=0)
             flip[pl.ds(pl.multiple_of(p * LANES, LANES), LANES), :] = y.T
             return 0
@@ -393,7 +446,7 @@
         def mix(j, _):
             normal = flip[pl.ds(j, channels, stride=ci), :].astype(BF16)
             linear = lax.dot_general(
-                normal, w_out[...], (((0,), (0,)), ((), ())), preferred_element_type=F32
+                normal, weights[...], (((0,), (0,)), ((), ())), preferred_element_type=F32
             )
             flop[pl.ds(j, ti, stride=ci), :] = linear[0:ti]
             return 0
@@ -422,14 +475,17 @@
         for m in range(nch):
             swap(m).wait_recv()
 
-    first = [(0, 0), (1, 0), (0, 1), (1, 1)]
+    first = [(0, 0), (1, 0)]
+    load.wait()
     for chunk in first:
         front(*chunk)
     pl.semaphore_wait(barrier, 2 * nq - 1 + 2 * ahead)
     plan = [
         (z_first,),
         (send1, 1, 0),
+        (front, 0, 1),
         (send1, 0, 1),
+        (front, 1, 1),
         (front, 0, 2),
         (enter, 1, 0),
         (send1, 1, 1),
@@ -486,10 +542,11 @@
         (finish, 2),
         (product, 4),
         (product, 5),
+        (turn_at_site, 5),
         (turn_and_send, 3),
+        (turn_and_return, 5),
         (turn_and_send, 4),
         (finish, 3),
-        (turn_and_send, 5),
         (finish, 4),
         (finish, 5),
     ]
@@ -532,9 +589,11 @@
     return pl.pallas_call(
         functools.partial(triangle_kernel, nz),
         out_shape=jax.ShapeDtypeStruct((ti, tj, cz), BF16),
-        in_specs=[vmem, smem] + [vmem] * 5 + [smem] + [vmem] * 2,
+        in_specs=[pl.BlockSpec(memory_space=pl.ANY), smem] + [vmem] * 5 + [smem] + [vmem] * 2,
         out_specs=vmem,
         scratch_shapes=[
+            pltpu.VMEM((ti, tj, cz), BF16),
+            sem,
             pltpu.VMEM((ti, LANES, cz), BF16),
             pltpu.VMEM((2, 2 * channels, cz), BF16),
             pltpu.VMEM((2, 2 * channels, LANES), F32),
@@ -542,6 +601,8 @@
             pltpu.VMEM((channels * ci, LANES), F32),
             pltpu.VMEM((ti * ci, cz), F32),
             pltpu.VMEM((nq, LANES), F32),
+            pltpu.VMEM((nq, LANES), F32),
+            pltpu.VMEM((channels, cz), BF16),
             pltpu.VMEM((2, nch, nq, nz, ci, LANES), BF16),
             pltpu.VMEM((nq, nz, ci, LANES), BF16),
             pltpu.VMEM((2, nch, nq, nz, ci, LANES), BF16),
@@ -552,6 +613,8 @@
             pltpu.VMEM((nch, nz, 2, ti, nz * ci), BF16),
             pltpu.VMEM((nch, nq, ti, LANES), BF16),
             pltpu.VMEM((nch, nq, ti, LANES), BF16),
+            pltpu.VMEM((nq, ti, LANES), BF16),
+            sem,
             sem,
             sem((2, nch)),
             sem,

time: 178 us -> 174 us (0.978)
  Pallas kernels: 174 us -> 170 us
    pallas_call x1, Pallas kernels: 174 us -> 170 us  [local(): pl.pallas_call(functools.partial(triangle_kernel, nz), out_shape=jax.Shap...]
where the time goes in v6:
time: 174 us; the launch traced here: 173 us
  Pallas kernels  170 us (98%)
  local copies, waits for them, and re-layouts  3.22 us (2%)
    pallas_call x1, Pallas kernels, local(): pl.pallas_call(functools.partial(triangle_kernel, nz), out_shape=jax.Shap...  170 us

profile of v6, /device:TPU:1, one launch (start us, length us, event | category | flops | bytes accessed | tf_op | source)
XLA Modules:
  0.0 173.3 jit_solution(1789224472053587715)
XLA Ops:
  0.0 170.1 %shard_map.100 = bf16[96,96,128]{2,1,0:T(8,128)(2,1)} custom-call(bf16[96,96,128]{2,1,0:T(8,128)(2,1)} %pair_in.1, s32[1536]{0:T(1024)} %valid.1, f32[1,128]{1,0:T(1,128)} %bitcast.5, bf16[128,512]{1,0:T(8,128)(2,1)} %w_in.1, f32[1,512]{1,0:T(1,128)} %bitcast.4, bf16[128,128]{1,0:T(8,128)(2,1)} %w_gate.1, f32[1,128]{1,0:T(1,128)} %bitcast.6, f32[128]{0:T(128)} %gain.1, ...), custom_call_target="tpu_custom_call" | custom-call | tf_op jit(solution)/shard_map/pallas_call | solution.py:589
  170.1 3.2 %copy.12 = bf16[96,96,128]{2,1,0:T(8,128)(2,1)} copy(bf16[96,96,128]{2,1,0:T(8,128)(2,1)} %shard_map.100) | data formatting | bytes 4718592

commit v7 on v6

--- a/solution.py
+++ b/solution.py
@@ -192,7 +192,7 @@
                 )
             return 0
 
-        lax.fori_loop(0, ci // 4, step, 0, unroll=2)
+        lax.fori_loop(0, ci // 4, step, 0, unroll=True)
 
         def pack(p, _):
             for ch in range(nz):
@@ -201,7 +201,7 @@
                 ].astype(BF16)
             return 0
 
-        lax.fori_loop(0, nq, pack, 0, unroll=2)
+        lax.fori_loop(0, nq, pack, 0, unroll=4)
 
     def gates(q, _):
         rows = nrm[pl.ds(4 * q, 4)].reshape(4 * LANES, cz)
@@ -278,7 +278,7 @@
                         zs[arr, m, place, :, lanes] = joined[n].astype(BF16)
             return 0
 
-        lax.fori_loop(0, nz, step, 0)
+        lax.fori_loop(0, nz, step, 0, unroll=2)
         if at_site:
             return
         for place in far_first:
@@ -359,7 +359,7 @@
                 store_block(i, h, rows, block.astype(BF16))
             return 0
 
-        lax.fori_loop(0, 6, step, 0)
+        lax.fori_loop(0, 6, step, 0, unroll=2)
 
     def to_plane(m, dst, sem):
         def go(t, _):
@@ -441,7 +441,7 @@
             flip[pl.ds(pl.multiple_of(p * LANES, LANES), LANES), :] = y.T
             return 0
 
-        lax.fori_loop(0, nq, scaled, 0, unroll=4)
+        lax.fori_loop(0, nq, scaled, 0, unroll=True)
 
         def mix(j, _):
             normal = flip[pl.ds(j, channels, stride=ci), :].astype(BF16)
@@ -451,7 +451,7 @@
             flop[pl.ds(j, ti, stride=ci), :] = linear[0:ti]
             return 0
 
-        lax.fori_loop(0, ci, mix, 0, unroll=4)
+        lax.fori_loop(0, ci, mix, 0, unroll=True)
 
         def emit(n, _):
             rows, columns = pl.ds(8 * n, 8), slice(m * ci, (m + 1) * ci)
@@ -486,42 +486,42 @@
         (front, 0, 1),
         (send1, 0, 1),
         (front, 1, 1),
+        (send1, 1, 1),
         (front, 0, 2),
         (enter, 1, 0),
-        (send1, 1, 1),
+        (send1, 0, 2),
         (front, 0, 3),
+        (then_plane,),
         (front, 1, 2),
-        (then_plane,),
         (enter, 0, 1),
-        (send1, 0, 2),
+        (send1, 0, 3),
         (front, 0, 4),
         (pass_on, 0, 1),
         (enter, 1, 1),
-        (send1, 0, 3),
+        (send1, 1, 2),
         (front, 0, 5),
         (enter, 0, 2),
-        (send1, 1, 2),
+        (send1, 0, 4),
         (enter, 0, 0),
         (join_swap, 0),
         (join_swap, 1),
         (front, 1, 3),
         (pass_on, 1, 1),
         (enter, 0, 3),
-        (send1, 0, 4),
+        (send1, 0, 5),
         (front, 1, 4),
         (join_swap, 2),
         (all_gates,),
         (enter, 1, 2),
-        (send1, 0, 5),
+        (send1, 1, 3),
         (front, 1, 5),
         (enter, 0, 4),
-        (send1, 1, 3),
+        (send1, 1, 4),
         (join_swap, 3),
         (enter, 0, 5),
-        (send1, 1, 4),
+        (send1, 1, 5),
         (pass_on, 2, 1),
         (enter, 1, 3),
-        (send1, 1, 5),
         (join_swap, 4),
         (enter, 1, 4),
         (join_swap, 5),
@@ -537,12 +537,12 @@
         (turn_and_send, 1),
         (finish, 0),
         (turn_and_send, 2),
+        (product, 3),
+        (product, 4),
         (finish, 1),
-        (product, 3),
-        (finish, 2),
-        (product, 4),
         (product, 5),
         (turn_at_site, 5),
+        (finish, 2),
         (turn_and_send, 3),
         (turn_and_return, 5),
         (turn_and_send, 4),

time: 174 us -> 168 us (0.966)
  Pallas kernels: 170 us -> 164 us
    pallas_call x1, Pallas kernels: 170 us -> 164 us  [local(): pl.pallas_call(functools.partial(triangle_kernel, nz), out_shape=jax.Shap...]
where the time goes in v7:
time: 168 us
  Pallas kernels  164 us (98%)
  local copies, waits for them, and re-layouts  3.22 us (2%)
    pallas_call x1, Pallas kernels, local(): pl.pallas_call(functools.partial(triangle_kernel, nz), out_shape=jax.Shap...  164 us

profile of v7, /device:TPU:1, one launch (start us, length us, event | category | flops | bytes accessed | tf_op | source)
XLA Modules:
  0.0 167.5 jit_solution(15010230977228315003)
XLA Ops:
  0.0 164.3 %shard_map.100 = bf16[96,96,128]{2,1,0:T(8,128)(2,1)} custom-call(bf16[96,96,128]{2,1,0:T(8,128)(2,1)} %pair_in.1, s32[1536]{0:T(1024)} %valid.1, f32[1,128]{1,0:T(1,128)} %bitcast.5, bf16[128,512]{1,0:T(8,128)(2,1)} %w_in.1, f32[1,512]{1,0:T(1,128)} %bitcast.4, bf16[128,128]{1,0:T(8,128)(2,1)} %w_gate.1, f32[1,128]{1,0:T(1,128)} %bitcast.6, f32[128]{0:T(128)} %gain.1, ...), custom_call_target="tpu_custom_call" | custom-call | tf_op jit(solution)/shard_map/pallas_call | solution.py:589
  164.3 3.2 %copy.12 = bf16[96,96,128]{2,1,0:T(8,128)(2,1)} copy(bf16[96,96,128]{2,1,0:T(8,128)(2,1)} %shard_map.100) | data formatting | bytes 4718592

commit v8 on v7

--- a/solution.py
+++ b/solution.py
@@ -598,8 +598,8 @@
             pltpu.VMEM((2, 2 * channels, cz), BF16),
             pltpu.VMEM((2, 2 * channels, LANES), F32),
             pltpu.VMEM((ti, tj, cz), F32),
-            pltpu.VMEM((channels * ci, LANES), F32),
-            pltpu.VMEM((ti * ci, cz), F32),
+            pltpu.VMEM(((channels + 1) * ci, LANES), F32),
+            pltpu.VMEM(((ti + 1) * ci, cz), F32),
             pltpu.VMEM((nq, LANES), F32),
             pltpu.VMEM((nq, LANES), F32),
             pltpu.VMEM((channels, cz), BF16),

time: 168 us -> 168 us (level)
  no operation moved by 1% of the time
where the time goes in v8:
time: 168 us
  Pallas kernels  164 us (98%)
  local copies, waits for them, and re-layouts  3.22 us (2%)
    pallas_call x1, Pallas kernels, local(): pl.pallas_call(functools.partial(triangle_kernel, nz), out_shape=jax.Shap...  164 us

profile of v8, /device:TPU:1, one launch (start us, length us, event | category | flops | bytes accessed | tf_op | source)
XLA Modules:
  0.0 167.6 jit_solution(14045664780178509190)
XLA Ops:
  0.0 164.4 %shard_map.100 = bf16[96,96,128]{2,1,0:T(8,128)(2,1)} custom-call(bf16[96,96,128]{2,1,0:T(8,128)(2,1)} %pair_in.1, s32[1536]{0:T(1024)} %valid.1, f32[1,128]{1,0:T(1,128)} %bitcast.5, bf16[128,512]{1,0:T(8,128)(2,1)} %w_in.1, f32[1,512]{1,0:T(1,128)} %bitcast.4, bf16[128,128]{1,0:T(8,128)(2,1)} %w_gate.1, f32[1,128]{1,0:T(1,128)} %bitcast.6, f32[128]{0:T(128)} %gain.1, ...), custom_call_target="tpu_custom_call" | custom-call | tf_op jit(solution)/shard_map/pallas_call | solution.py:589
  164.4 3.2 %copy.12 = bf16[96,96,128]{2,1,0:T(8,128)(2,1)} copy(bf16[96,96,128]{2,1,0:T(8,128)(2,1)} %shard_map.100) | data formatting | bytes 4718592
